TPU v7x, 512 devices: a whole 4x4x16 slice. The times are simulated.
512 devices in a mesh: gx: 64 (over x, z), gy: 8 (over y, core).
Axes of the slice: x: 4, y: 4, z: 16, core: 2. Of those that a mesh axis runs over, the one named last changes fastest.
Arguments:
- snapshot: bfloat16 [3, 512, 128, 1024], P(None, 'gx', 'gy'), may hold values from -6 to 6
- basis: bfloat16 [3, 64, 16, 128, 512], P(None, 'gx', 'gy'), may hold values from -3000 to 3000
- taps: bfloat16 [3, 17], replicated, may hold values from 0.099609375 to 1
Outputs:
- new_modes: bfloat16 [3, 64, 16, 128, 512], P(None, 'gx', 'gy')
- new_mode: float32 [3, 64, 16, 128], P(None, 'gx', 'gy')
- factor: float32 [513, 513], replicated
All inputs are finite; a program needn't handle non-finite values.
Results may differ from a plain program's by a relative error of at most 0.0012.
The roundings to bfloat16 on the way count: a program that leaves them out, or rounds other values in their place, can miss the bound.
Values sent between devices are 32-bit elements; how exact they have to be, the bound alone decides.
A program may use at most 64 MiB of HBM per device.

v0:
```python
import jax
import jax.numpy as jnp
from jax import lax
from jax.sharding import PartitionSpec as P

STRIDE = 8


def padded(block, sides, width, periodic):
    for axis, dim in sides:
        count = lax.axis_size(axis)
        forward = [(i, i + 1) for i in range(count - 1)]
        if periodic:
            forward.append((count - 1, 0))
        backward = [(target, source) for source, target in forward]
        low = lax.ppermute(
            lax.slice_in_dim(block, block.shape[dim] - width, None, axis=dim), axis, forward
        )
        high = lax.ppermute(lax.slice_in_dim(block, 0, width, axis=dim), axis, backward)
        block = jnp.concatenate([low, block, high], axis=dim)
    return block


def band(taps_row, length, out_len, shift, wrap):
    rows = jnp.arange(length, dtype=jnp.int32)[:, None]
    cols = jnp.arange(out_len, dtype=jnp.int32)[None, :]
    lag = rows - STRIDE * cols + shift
    if wrap:
        lag = lag % length
    hits = lag[:, :, None] == jnp.arange(2 * STRIDE + 1, dtype=jnp.int32)[None, None, :]
    return jnp.sum(jnp.where(hits, taps_row[None, None, :], jnp.zeros((), taps_row.dtype)), axis=-1)


def local(snapshot, basis, taps):
    comps, cells_x, cells_y, cells_z = snapshot.shape
    modes = basis.shape[-1]
    flat_rows = basis.reshape(-1, modes)
    total = flat_rows.shape[0] * lax.axis_size("gx") * lax.axis_size("gy")
    matrix_z = band(taps[2], cells_z, cells_z // STRIDE, STRIDE, True)
    along_z = jnp.dot(snapshot.reshape(-1, cells_z), matrix_z, preferred_element_type=jnp.float32)
    along_z = along_z.reshape(comps, cells_x, cells_y, cells_z // STRIDE)
    padded_y = padded(along_z, (("gy", 2),), STRIDE, False)
    matrix_y = band(taps[1], cells_y + 2 * STRIDE, cells_y // STRIDE, 0, False).astype(jnp.float32)
    along_y = jnp.einsum("cxyz,yf->cxfz", padded_y, matrix_y, precision=lax.Precision.HIGHEST)
    padded_x = padded(along_y, (("gx", 1),), STRIDE, True)
    matrix_x = band(taps[0], cells_x + 2 * STRIDE, cells_x // STRIDE, 0, False).astype(jnp.float32)
    along_x = jnp.einsum("cxyz,xf->cfyz", padded_x, matrix_x, precision=lax.Precision.HIGHEST)
    filtered = along_x.astype(jnp.bfloat16).reshape(-1)
    stack = jnp.concatenate([flat_rows, filtered[:, None]], axis=1)
    gram = lax.psum(
        jnp.einsum("rk,rj->kj", stack, stack, preferred_element_type=jnp.float32), ("gx", "gy")
    )
    gram = gram / total
    lower = jnp.linalg.cholesky(gram)
    solved = lax.linalg.triangular_solve(
        lower, stack.astype(jnp.float32), left_side=False, lower=True, transpose_a=True
    )
    new_modes = solved[:, :modes].astype(jnp.bfloat16).reshape(basis.shape)
    new_mode = solved[:, modes].reshape(basis.shape[:-1])
    return (new_modes, new_mode, lower.T)


def solution(mesh):
    in_specs = (P(None, "gx", "gy", None), P(None, "gx", "gy", None, None), P())
    out_specs = (P(None, "gx", "gy", None, None), P(None, "gx", "gy", None), P())
    return jax.shard_map(local, mesh=mesh, in_specs=in_specs, out_specs=out_specs, check_vma=False)
```

profile of v0, /device:TPU:1, one launch (start us, length us, event | category | flops | bytes accessed | tf_op | source)
XLA Modules:
  0.0 709.4 jit_solution(6518800129823269705)
XLA Ops:
  7.2 0.8 slice_bitcast_fusion.14
  8.3 0.9 fusion.1
  9.2 0.4 convolution_bitcast_fusion
  9.8 4.6 collective-permute-start
  14.4 5.5 collective-permute-start.1
  20.1 0.7 collective-permute-done.1
  21.1 3.1 collective-permute-start.2
  24.1 11.7 %collective-permute-start.3 = (f32[3,8,2,128]{3,2,1,0:T(2,128)S(1)}, f32[3,8,2,128]{3,2,1,0:T(2,128)S(1)}, u32[]{:S(2)}, u32[]{:S(2)}) collective-permute-start(f32[3,8,2,128]{3,2,1,0:T(2,128)S(1)} %convolution_bitcast_fusion.1), channel_id=1, source_target_pairs={{8,0},{16,8},{24,16},{32,24},{40,32},{48,40},{56,48},{64,56},{72,6... | collective-permute-start | bytes 73736 | tf_op jit(solution)/shard_map/ppermute | solution.py:19
  35.9 0.8 collective-permute-done.3
  37.3 1.9 fusion.25
  39.3 1.4 fusion.24
  40.7 462.9 %all-reduce.5.cloned.1.call-done = f32[513,513]{0,1:T(8,128)} async-done(((f32[513,513]{0,1:T(8,128)}), f32[513,513]{0,1:T(8,128)}) %all-reduce.5.cloned.1.call-update) | async-done | bytes 1052692 | tf_op jit(solution)/shard_map/psum | solution.py:50
  503.6 2.5 broadcast_multiply_fusion
  506.1 1.9 copy.56
  508.3 1.0 copy-done.4
  509.3 0.5 cholesky.348
  509.8 11.7 %cholesky.131 = f32[128,128]{1,0:T(8,128)S(1)} custom-call(f32[128,128]{1,0:T(8,128)S(1)} %cholesky.333), custom_call_target="Cholesky" | custom-call | tf_op jit(solution)/shard_map/jit(cholesky)/cholesky | solution.py:54
  521.6 9.8 %custom-call.35 = f32[1,128,128]{1,2,0:T(8,128)S(1)} custom-call(f32[1,128,128]{2,1,0:T(8,128)S(1)} %get-tuple-element.47), custom_call_target="InvertDiagBlocksLowerTriangular" | custom-call | tf_op jit(solution)/shard_map/jit(cholesky)/cholesky | solution.py:54
  531.5 1.4 constant_dynamic-update-slice_fusion.2
  532.9 1.4 convolution_subtract_fusion.3
  534.3 11.9 %cholesky.264 = f32[128,128]{1,0:T(8,128)S(1)} custom-call(f32[128,128]{1,0:T(8,128)S(1)} %cholesky.337), custom_call_target="Cholesky" | custom-call | tf_op jit(solution)/shard_map/jit(cholesky)/cholesky | solution.py:54
  546.2 9.8 %custom-call.36 = f32[1,128,128]{1,2,0:T(8,128)S(1)} custom-call(f32[1,128,128]{2,1,0:T(8,128)S(1)} %get-tuple-element.44), custom_call_target="InvertDiagBlocksLowerTriangular" | custom-call | tf_op jit(solution)/shard_map/jit(cholesky)/cholesky | solution.py:54
  556.0 0.4 convolution_dynamic-update-slice_fusion
  556.4 1.3 convolution_subtract_fusion.4
  557.7 11.7 %cholesky.285 = f32[128,128]{1,0:T(8,128)S(1)} custom-call(f32[128,128]{1,0:T(8,128)S(1)} %cholesky.342), custom_call_target="Cholesky" | custom-call | tf_op jit(solution)/shard_map/jit(cholesky)/cholesky | solution.py:54
  569.5 9.8 %custom-call.37 = f32[1,128,128]{1,2,0:T(8,128)S(1)} custom-call(f32[1,128,128]{2,1,0:T(8,128)S(1)} %get-tuple-element.41), custom_call_target="InvertDiagBlocksLowerTriangular" | custom-call | tf_op jit(solution)/shard_map/jit(cholesky)/cholesky | solution.py:54
  579.5 1.3 convolution_subtract_fusion.5
  580.8 11.9 %cholesky.304 = f32[128,128]{1,0:T(8,128)S(1)} custom-call(f32[128,128]{1,0:T(8,128)S(1)} %cholesky.347), custom_call_target="Cholesky" | custom-call | tf_op jit(solution)/shard_map/jit(cholesky)/cholesky | solution.py:54
  592.8 9.8 %custom-call.38 = f32[1,128,128]{1,2,0:T(8,128)S(1)} custom-call(f32[1,128,128]{2,1,0:T(8,128)S(1)} %get-tuple-element.38), custom_call_target="InvertDiagBlocksLowerTriangular" | custom-call | tf_op jit(solution)/shard_map/jit(cholesky)/cholesky | solution.py:54
  602.9 0.6 multiply_reduce_fusion
  604.9 0.7 compare_reduce_fusion.1
  605.6 0.7 compare_reduce_fusion
  606.3 0.6 compare_reduce_fusion.2
  609.5 1.3 fusion.20
  610.8 0.5 triangular_solve.195
  611.3 10.1 %while.1 = (s32[]{:T(128)}, f32[513,513]{1,0:T(8,128)S(1)}, s32[4,2]{0,1:T(2,128)S(1)}, f32[4,128,128]{2,1,0:T(8,128)}, s32[]{:T(128)}) while((s32[]{:T(128)}, f32[513,513]{1,0:T(8,128)S(1)}, s32[4,2]{0,1:T(2,128)S(1)}, f32[4,128,128]{2,1,0:T(8,128)}, s32[]{:T(128)}) %tuple.44), condition=%wide.while_cond, body=%wide.while_body.sunk | while | flops 2 | bytes 132705 | solution.py:55
  611.3 0.5 fusion.82
  611.9 1.9 bitcast_dynamic-update-slice_fusion.2
  613.9 0.5 fusion.82
  614.4 1.9 bitcast_dynamic-update-slice_fusion.2
  616.4 0.5 fusion.82
  616.9 1.9 bitcast_dynamic-update-slice_fusion.2
  618.9 0.5 fusion.82
  619.4 1.9 bitcast_dynamic-update-slice_fusion.2
  621.4 0.7 fusion.52
  622.1 1.0 pad_maximum_fusion.3
  623.1 49.1 %custom-call.39 = f32[5,128,128]{1,2,0:T(8,128)S(1)} custom-call(f32[5,128,128]{2,1,0:T(8,128)S(1)} %pad_maximum_fusion.3), custom_call_target="InvertDiagBlocksLowerTriangular" | custom-call | tf_op jit(solution)/shard_map/triangular_solve | solution.py:55
  672.2 2.1 bitcast_convert_fusion
  674.3 0.5 triangular_solve.209
  674.8 2.0 convolution_subtract_fusion.1
  676.8 2.1 fusion.73
  678.9 1.2 copy.57
  680.1 2.3 convolution_subtract_fusion.2
  682.4 2.1 fusion.72
  684.5 1.9 copy.59
  686.4 3.1 convolution_subtract_fusion
  689.5 2.1 fusion.71
  691.6 1.9 copy.66
  693.5 2.0 fusion.17
  695.6 0.9 fusion.28
  696.5 0.6 triangular_solve.193
  697.1 1.1 copy.77
  698.2 2.9 copy.69
  701.2 1.0 pad_maximum_fusion.1
  (60 shorter events, 3.0 us)
Async XLA Ops:
  7.2 2.1 copy-start
  7.2 496.4 %all-reduce.5.cloned.1.call-start = ((), (), s32[]{:S(2)}) async-start(), calls=%async_computation | async-start | bytes 2662400 | tf_op jit(solution)/shard_map/psum | solution.py:50
  9.2 28.1 %copy-start.5 = (bf16[3,1,2,128,512]{4,3,2,1,0:T(8,128)(2,1)S(1)}, bf16[3,1,2,128,512]{4,3,2,1,0:T(8,128)(2,1)}, u32[]{:S(2)}) copy-start(bf16[3,1,2,128,512]{4,3,2,1,0:T(8,128)(2,1)} %param.4) | copy-start | bytes 2359300
  9.8 10.3 %collective-permute-start = (f32[3,8,8,128]{3,2,1,0:T(8,128)S(1)}, f32[3,8,8,128]{3,2,1,0:T(8,128)S(1)}, u32[]{:S(2)}, u32[]{:S(2)}) collective-permute-start(f32[3,8,8,128]{3,2,1,0:T(8,128)S(1)} %get-tuple-element.35), channel_id=1, source_target_pairs={{0,1},{1,2},{2,3},{3,4},{4,5},{5,6},{6,7},{8,9},{9,10},{10,11},{11... | collective-permute-start | bytes 294920 | tf_op jit(solution)/shard_map/ppermute | solution.py:16
  14.4 6.4 collective-permute-start.1
  21.1 14.9 %collective-permute-start.2 = (f32[3,8,2,128]{3,2,1,0:T(2,128)S(1)}, f32[3,8,2,128]{3,2,1,0:T(2,128)S(1)}, u32[]{:S(2)}, u32[]{:S(2)}) collective-permute-start(f32[3,8,2,128]{3,2,1,0:T(2,128)S(1)} %convolution_bitcast_fusion.1), channel_id=1, source_target_pairs={{0,8},{8,16},{16,24},{24,32},{32,40},{40,48},{48,56},{56,64},{64,7... | collective-permute-start | bytes 73736 | tf_op jit(solution)/shard_map/ppermute | solution.py:16
  24.1 12.6 %collective-permute-start.3 = (f32[3,8,2,128]{3,2,1,0:T(2,128)S(1)}, f32[3,8,2,128]{3,2,1,0:T(2,128)S(1)}, u32[]{:S(2)}, u32[]{:S(2)}) collective-permute-start(f32[3,8,2,128]{3,2,1,0:T(2,128)S(1)} %convolution_bitcast_fusion.1), channel_id=1, source_target_pairs={{8,0},{16,8},{24,16},{32,24},{40,32},{48,40},{56,48},{64,56},{72,6... | collective-permute-start | bytes 73736 | tf_op jit(solution)/shard_map/ppermute | solution.py:19
  506.1 1.9 copy-start.2
  508.2 1.1 copy-start.4
  621.4 53.5 %copy-start.3 = (f32[513,513]{1,0:T(8,128)}, f32[513,513]{1,0:T(8,128)S(1)}, u32[]{:S(2)}) copy-start(f32[513,513]{1,0:T(8,128)S(1)} %get-tuple-element.109) | copy-start | bytes 3158032
  672.2 2.6 copy-start.9
  674.8 5.2 copy-start.1
  698.2 3.0 copy-start.6
  698.2 2.9 copy-start.7
  698.2 2.9 copy-start.8
Sparse Core Ops, SparseCore 0:
  39.4 464.2 all-reduce.4
where the time goes:
time: 720 us; the launch traced here: 709 us
  waiting for transfers between devices  464 us (64%)
  other arithmetic  149 us (21%)
  matrix products  26.7 us (4%)
  local copies, waits for them, and re-layouts  25.8 us (4%)
  starting transfers between devices  24.9 us (3%)
  between operations  18.8 us (3%)
    psum x1, waiting for transfers between devices, local(): lax.psum(jnp.einsum('rk,rj->kj', stack, stack, preferred_element_type=jnp...  463 us
    another operation x16, other arithmetic, local(): lower = jnp.linalg.cholesky(gram)  89.2 us
    another operation x8, other arithmetic, local(): lax.linalg.triangular_solve(lower, stack.astype(jnp.float32), left_side=F...  52.8 us
    another operation x8, matrix products, local(): lax.linalg.triangular_solve(lower, stack.astype(jnp.float32), left_side=F...  17.8 us
    ppermute x2, starting transfers between devices, padded(): lax.ppermute(lax.slice_in_dim(block, 0, width, axis=dim), axis, backward)  17.2 us
  transfers between devices with their start and end apart: 5, of which 3 were waited for; matrix products, arithmetic and copies ran while one was open for 0% of the time, Pallas kernels for 0%

commit v1 on v0

v1 whole, which is shorter than its diff:
```python
import functools
import jax, jax.numpy as jnp
from jax import lax
from jax.sharding import PartitionSpec as P
from jax.experimental import pallas as pl
from jax.experimental.pallas import tpu as pltpu

F32, BF16 = jnp.float32, jnp.bfloat16
B = 128
HI = lax.Precision.HIGHEST

def lane_splat(tile, lane):
    return jnp.broadcast_to(tile[:, lane:lane + 1], (8, B))

def row_splat(tile, row):
    return jnp.broadcast_to(tile[row:row + 1, :], (8, B))

def recip(x):
    r = pl.reciprocal(x, approx=True)
    r = r * (2.0 - x * r)
    return r

def factor_block(a):
    sub = lax.broadcasted_iota(jnp.int32, (8, B), 0)
    lane = lax.broadcasted_iota(jnp.int32, (8, B), 1)
    n = B // 8
    a = list(a)
    z = [jnp.where(lane == 8 * t + sub, 1.0, 0.0) for t in range(n)]
    diag = [lane_splat(a[0], j) for j in range(8)]
    for p in range(n):
        cols = diag
        inv = []
        row = {}
        pivots = jnp.ones((8, B), F32)
        for k in range(8):
            pivot = row_splat(cols[k], k)
            pivots = jnp.where(sub == k, pivot, pivots)
            r = recip(pivot)
            inv.append(r)
            m = jnp.where(sub > k, cols[k] * r, 0.0)
            for j in range(k + 1, 8):
                row[k, j] = row_splat(cols[j], k)
                cols[j] = cols[j] - m * row[k, j]
            if k < 7:
                a[p] = a[p] - m * row_splat(a[p], k)
                z[p] = z[p] - m * row_splat(z[p], k)
        mult = {}
        for t in range(p + 1, n):
            c = [lane_splat(a[t], 8 * p + j) for j in range(8)]
            for k in range(8):
                m = c[k] * inv[k]
                mult[t, k] = m
                for j in range(k + 1, 8):
                    c[j] = c[j] - m * row[k, j]
            if t == p + 1:
                diag = []
                for j in range(8):
                    d = lane_splat(a[t], 8 * t + j)
                    for k in range(8):
                        d = d - mult[t, k] * row_splat(c[k], j)
                    diag.append(d)
        for k in range(8):
            if p + 1 < n:
                ua, uz = row_splat(a[p], k), row_splat(z[p], k)
            for t in range(p + 1, n):
                a[t] = a[t] - mult[t, k] * ua
                z[t] = z[t] - mult[t, k] * uz
        s = lax.rsqrt(pivots)
        a[p] = jnp.where(lane >= 8 * p + sub, a[p] * s, 0.0)
        z[p] = z[p] * s
    return a, z

PAIRS = [(b, c) for b in range(4) for c in range(b, 4)]
INDEX = {pair: i for i, pair in enumerate(PAIRS)}

def nn(x, y): return lax.dot_general(x, y, (((1,), (0,)), ((), ())), precision=HI, preferred_element_type=F32)
def tn(x, y): return lax.dot_general(x, y, (((0,), (0,)), ((), ())), precision=HI, preferred_element_type=F32)
def nt(x, y): return lax.dot_general(x, y, (((1,), (1,)), ((), ())), precision=HI, preferred_element_type=F32)
def nt16(x, y): return lax.dot_general(x, y, (((1,), (1,)), ((), ())), preferred_element_type=F32)

def split(x):
    hi = x.astype(BF16)
    return hi, (x - hi.astype(F32)).astype(BF16)

def k2_kernel(total, nblk, g_ref, f_ref, basis_ref, modes_ref, mode_ref, factor_ref, s_ref, zw_ref, zh_ref, zl_ref):
    scale = 1.0 / total
    for i in range(10):
        s_ref[i] = g_ref[i * B:(i + 1) * B, :] * scale
    grow = g_ref[1280:1288, :] * scale
    factor_ref[...] = jnp.zeros_like(factor_ref)
    zh_ref[...] = jnp.zeros_like(zh_ref)
    zl_ref[...] = jnp.zeros_like(zl_ref)
    zw_ref[...] = jnp.zeros_like(zw_ref)
    for b in range(nblk):
        blk = INDEX[b, b]
        a, z = factor_block([s_ref[blk, 8 * t:8 * t + 8, :] for t in range(16)])
        w = jnp.concatenate(z, axis=0)
        lo = b * B
        factor_ref[lo:lo + B, lo:lo + B] = jnp.concatenate(a, axis=0)
        zw_ref[lo:lo + B, lo:lo + B] = w
        r = {}
        for c in range(b + 1, 4):
            r[c] = nn(w, s_ref[INDEX[b, c]])
            factor_ref[lo:lo + B, c * B:(c + 1) * B] = r[c]
        if b:
            zw_ref[lo:lo + B, 0:lo] = nn(w, zw_ref[lo:lo + B, 0:lo])
        zrow = zw_ref[lo:lo + B, 0:lo + B]
        for i in range(b + 1, 4):
            for c in range(i, 4):
                s_ref[INDEX[i, c]] = s_ref[INDEX[i, c]] - tn(r[i], r[c])
            zw_ref[i * B:(i + 1) * B, 0:lo + B] = zw_ref[i * B:(i + 1) * B, 0:lo + B] - tn(r[i], zrow)
        zh, zl = split(zrow)
        zh_ref[lo:lo + B, 0:lo + B] = zh
        zl_ref[lo:lo + B, 0:lo + B] = zl
        out = nt16(basis_ref[:, 0:lo + B], zh_ref[lo:lo + B, 0:lo + B]) + nt16(basis_ref[:, 0:lo + B], zl_ref[lo:lo + B, 0:lo + B])
        modes_ref[:, lo:lo + B] = out.astype(BF16)
    g4 = jnp.concatenate([grow[i:i + 1, :] for i in range(4)], axis=1)
    g8 = jnp.broadcast_to(g4, (8, 512))
    zall = zw_ref[...]
    rcol = nt(zall, g8)
    rrow = nt(g8, zall)
    v = nn(rrow, zall)
    d2 = grow[4:5, 0:1] - jnp.sum(rrow[0:1] * rrow[0:1], axis=1, keepdims=True)
    inv_d = lax.rsqrt(d2)
    factor_ref[0:512, 512:513] = rcol[:, 0:1]
    factor_ref[512:513, 512:513] = d2 * inv_d
    vh, vl = split(v)
    y = nt16(vh, basis_ref[...]) + nt16(vl, basis_ref[...])
    y6 = jnp.concatenate([y[0:1, i * B:(i + 1) * B] for i in range(6)], axis=0)
    mode_ref[...] = (f_ref[...] - y6) * inv_d

def k2(g, f, basis, total=393216.0, nblk=4, kern=k2_kernel):
    rows = basis.shape[0]
    return pl.pallas_call(
        functools.partial(kern, total, nblk),
        out_shape=(jax.ShapeDtypeStruct((rows, 512), BF16), jax.ShapeDtypeStruct((6, B), F32), jax.ShapeDtypeStruct((513, 513), F32)),
        in_specs=[pl.BlockSpec(memory_space=pltpu.VMEM)] * 3,
        out_specs=[pl.BlockSpec(memory_space=pltpu.VMEM)] * 3,
        scratch_shapes=[pltpu.VMEM((10, B, B), F32), pltpu.VMEM((512, 512), F32), pltpu.VMEM((512, 512), BF16), pltpu.VMEM((512, 512), BF16)],
        compiler_params=pltpu.CompilerParams(vmem_limit_bytes=40 << 20),
        name="factor",
    )(g, f, basis)

MESH = pl.DeviceIdType.MESH
NPLANE, NZR, CH = 16, 16, 48
PIECE = CH // NZR
ROWS = 2 * NPLANE * CH
NEAR = [(dx, dy) for dx in (0, 1, -1) for dy in (0, 1, -1) if (dx, dy) != (0, 0)]


def tap_tiles(taps, d, sub):
    def at(i):
        return jnp.broadcast_to(taps[d:d + 1, i:i + 1], (8, B))
    ahead = behind = jnp.zeros((8, B), F32)
    for s in range(8):
        ahead = jnp.where(sub == s, at(8 + s), ahead)
        behind = jnp.where(sub == s, at(s), behind)
    return ahead, behind, jnp.where(sub == 0, at(16), 0.0)


def reduce_kernel(taps_ref, snap_ref, basis_ref, gram_ref, filt_ref, band_ref, near_out, near_in, acc, recv_a, recv_b, chunk_ref, recv_c, piece_ref, ring_ref, full_ref, near_s, near_r, sa, ra, sb, rb, sc, rc, sd, rd, se, re, sf, rf):
    gx, gy = lax.axis_index("gx"), lax.axis_index("gy")
    x, z = gx // NZR, gx % NZR
    y, core = gy // 2, gy % 2
    plane = x * 4 + y

    def near_id(dx, dy):
        return ((gx + dx + 64) % 64, (gy + dy + 8) % 8)

    def plane_id(k):
        p = (plane + k) % NPLANE
        return ((p // 4) * NZR + z, (p % 4) * 2 + core)

    def z_id(k):
        return (x * NZR + (z + k) % NZR, gy)

    sibling = (gx, y * 2 + (1 - core))
    barrier = pltpu.get_barrier_semaphore()
    partners = [near_id(dx, dy) for dx, dy in NEAR] + [plane_id(k) for k in range(1, NPLANE)] + [z_id(k) for k in range(1, NZR)] + [sibling]
    for partner in partners:
        pl.semaphore_signal(barrier, inc=1, device_id=partner, device_id_type=MESH)

    sub = lax.broadcasted_iota(jnp.int32, (8, B), 0)
    lane = lax.broadcasted_iota(jnp.int32, (8, B), 1)
    taps = taps_ref[...].astype(F32)
    ahead, behind, last = tap_tiles(taps, 2, sub)
    for m in range(0, 128, 2):
        pair = []
        for t in (m, m + 1):
            tile = jnp.where(lane == t, ahead, 0.0)
            tile = jnp.where(lane == (t + 1) % 128, behind, tile)
            pair.append(jnp.where(lane == (t + 127) % 128, last, tile))
        band_ref[8 * m:8 * m + 16, :] = jnp.concatenate(pair, axis=0).astype(BF16)
    along_z = jnp.dot(snap_ref[...], band_ref[...], preferred_element_type=F32)
    ahead, behind, last = tap_tiles(taps, 0, sub)
    w_ahead = [row_splat(ahead, s) for s in range(8)]
    w_behind = [row_splat(behind, s) for s in range(8)]
    w_last = row_splat(last, 0)
    ahead, behind, last = tap_tiles(taps, 1, sub)
    sums = {}
    for dx in (0, 1, -1):
        for dy in (0, 1, -1):
            sums[dx, dy] = jnp.zeros((8, B), F32)
    for c in range(3):
        cell = [[along_z[(c * 8 + i) * 16 + 8 * h:(c * 8 + i) * 16 + 8 * h + 8, :] for i in range(8)] for h in range(2)]
        for dx in (0, 1, -1):
            half = []
            for h in range(2):
                if dx == -1:
                    half.append(w_last * cell[h][0])
                else:
                    w = w_ahead if dx == 0 else w_behind
                    v = w[0] * cell[h][0]
                    for i in range(1, 8):
                        v = v + w[i] * cell[h][i]
                    half.append(v)
            def put(dy, q, tile):
                total = jnp.sum(tile, axis=0, keepdims=True)
                sums[dx, dy] = jnp.where(sub == 2 * c + q, jnp.broadcast_to(total, (8, B)), sums[dx, dy])
            put(0, 0, ahead * half[0] + last * half[1])
            put(0, 1, behind * half[0] + ahead * half[1])
            put(1, 0, behind * half[1])
            put(-1, 1, last * half[0])
    for e, (dx, dy) in enumerate(NEAR):
        tile = sums[dx, dy]
        if dy == 1:
            tile = jnp.where(gy == 7, 0.0, tile)
        if dy == -1:
            tile = jnp.where(gy == 0, 0.0, tile)
        near_out[e] = tile
    pl.semaphore_wait(barrier, len(partners))

    def copy(src, dst, ssem, rsem, device):
        c = pltpu.make_async_remote_copy(src_ref=src, dst_ref=dst, send_sem=ssem, recv_sem=rsem, device_id=device, device_id_type=MESH)
        c.start()
        return c

    near = [copy(near_out.at[e], near_in.at[e], near_s.at[e], near_r.at[e], near_id(dx, dy)) for e, (dx, dy) in enumerate(NEAR)]

    at = 0
    for b in range(4):
        width = 512 - b * B
        part = lax.dot_general(basis_ref[:, b * B:(b + 1) * B], basis_ref[:, b * B:512], (((0,), (0,)), ((), ())), preferred_element_type=F32)
        for c in range(width // B):
            acc[at:at + B, :] = part[:, c * B:(c + 1) * B]
            at += B

    for c in near:
        c.wait()
    f = sums[0, 0]
    for e in range(len(NEAR)):
        f = f + near_in[e]
    f16 = f.astype(BF16)
    f = f16.astype(F32)
    filt_ref[...] = f[0:6, :]
    frow = jnp.concatenate([jnp.broadcast_to(f[i:i + 1, :], (8, B)) for i in range(6)], axis=1).astype(BF16)
    g = jnp.dot(frow, basis_ref[...], preferred_element_type=F32)
    sq = jnp.where(sub < 6, f * f, 0.0)
    ff = jnp.sum(jnp.sum(sq, axis=1, keepdims=True), axis=0, keepdims=True)
    tail = jnp.where(sub == 4, jnp.broadcast_to(ff, (8, B)), 0.0)
    for i in range(4):
        tail = jnp.where(sub == i, g[:, i * B:(i + 1) * B], tail)
    acc[1280:1288, :] = tail
    acc[1288:ROWS, :] = jnp.zeros((ROWS - 1288, B), F32)

    half = NPLANE * CH
    ca = copy(acc.at[pl.ds((1 - core) * half, half)], recv_a, sa, ra, sibling)
    ca.wait()
    recv_a[...] = recv_a[...] + acc[pl.ds(core * half, half), :]
    cb = []
    for k in range(1, NPLANE):
        p = (plane + k) % NPLANE
        cb.append(copy(recv_a.at[pl.ds(p * CH, CH)], recv_b.at[k - 1], sb.at[k - 1], rb.at[k - 1], plane_id(k)))
    total = recv_a[pl.ds(plane * CH, CH), :]
    for k in range(1, NPLANE):
        cb[k - 1].wait_recv()
        total = total + recv_b[k - 1]
    for i in range(NZR):
        chunk_ref[i] = total[i * PIECE:(i + 1) * PIECE, :]
    cc = []
    for k in range(1, NZR):
        cc.append(copy(chunk_ref.at[(z + k) % NZR], recv_c.at[k - 1], sc.at[k - 1], rc.at[k - 1], z_id(k)))
    total = chunk_ref[z]
    for k in range(1, NZR):
        cc[k - 1].wait_recv()
        total = total + recv_c[k - 1]
    piece_ref[...] = total
    cd = []
    for k in range(1, NZR):
        cd.append(copy(piece_ref, ring_ref.at[z], sd.at[k - 1], rd.at[k - 1], z_id(k)))
    ring_ref[z] = total
    for k in range(1, NZR):
        cd[k - 1].wait_recv()
    mine = recv_a.at[pl.ds(0, CH)]
    for c in cb:
        c.wait_send()
    for i in range(NZR):
        recv_a[i * PIECE:(i + 1) * PIECE, :] = ring_ref[i]
    ce = []
    for k in range(1, NPLANE):
        ce.append(copy(mine, full_ref.at[core, plane], se.at[k - 1], re.at[k - 1], plane_id(k)))
    full_ref[core, plane] = recv_a[0:CH, :]
    cf = [copy(mine, full_ref.at[core, plane], sf.at[0], rf.at[0], sibling)]
    for k in range(1, NPLANE):
        ce[k - 1].wait_recv()
        p = (plane - k + NPLANE) % NPLANE
        cf.append(copy(full_ref.at[core, p], full_ref.at[core, p], sf.at[k], rf.at[k], sibling))
    for c in cf:
        c.wait_recv()
    for i in range(2):
        for j in range(NPLANE):
            gram_ref[(i * NPLANE + j) * CH:(i * NPLANE + j + 1) * CH, :] = full_ref[i, j]
    for c in cc + cd + ce + cf:
        c.wait_send()


def reduced(taps, snap, basis):
    dma = pltpu.SemaphoreType.DMA
    return pl.pallas_call(
        reduce_kernel,
        out_shape=(jax.ShapeDtypeStruct((ROWS, B), F32), jax.ShapeDtypeStruct((6, B), F32)),
        in_specs=[pl.BlockSpec(memory_space=pltpu.VMEM)] * 3,
        out_specs=[pl.BlockSpec(memory_space=pltpu.VMEM)] * 2,
        scratch_shapes=[
            pltpu.VMEM((1024, B), BF16),
            pltpu.VMEM((8, 8, B), F32),
            pltpu.VMEM((8, 8, B), F32),
            pltpu.VMEM((ROWS, B), F32),
            pltpu.VMEM((NPLANE * CH, B), F32),
            pltpu.VMEM((NPLANE - 1, CH, B), F32),
            pltpu.VMEM((NZR, PIECE, B), F32),
            pltpu.VMEM((NZR - 1, PIECE, B), F32),
            pltpu.VMEM((PIECE, B), F32),
            pltpu.VMEM((NZR, PIECE, B), F32),
            pltpu.VMEM((2, NPLANE, CH, B), F32),
            dma((8,)), dma((8,)), dma, dma,
            dma((15,)), dma((15,)), dma((15,)), dma((15,)), dma((15,)), dma((15,)), dma((15,)), dma((15,)), dma((16,)), dma((16,)),
        ],
        compiler_params=pltpu.CompilerParams(vmem_limit_bytes=40 << 20, collective_id=0, has_side_effects=True),
        name="reduce",
    )(taps, snap, basis)


def local(snapshot, basis, taps):
    flat = basis.reshape(-1, basis.shape[-1])
    g, f = reduced(taps, snapshot.reshape(-1, snapshot.shape[-1]), flat)
    total = flat.shape[0] * lax.axis_size("gx") * lax.axis_size("gy")
    modes, mode, fac = k2(g, f, flat, float(total))
    return modes.reshape(basis.shape), mode.reshape(basis.shape[:-1]), fac


def solution(mesh):
    in_specs = (P(None, "gx", "gy", None), P(None, "gx", "gy", None, None), P())
    out_specs = (P(None, "gx", "gy", None, None), P(None, "gx", "gy", None), P())
    return jax.shard_map(local, mesh=mesh, in_specs=in_specs, out_specs=out_specs, check_vma=False)
```

time: 720 us -> 80.4 us (0.11); the launches traced: 709 us -> 80.2 us
  waiting for transfers between devices: 464 us -> 0 us
  other arithmetic: 149 us -> 0 us
  Pallas kernels: 0 us -> 76 us
  matrix products: 26.7 us -> 0 us
  starting transfers between devices: 24.9 us -> 0 us
  local copies, waits for them, and re-layouts: 25.8 us -> 3.53 us
  between operations: 18.8 us -> 0.66 us
    psum x1 -> x0, waiting for transfers between devices: 463 us -> none  [local(): lax.psum(jnp.einsum('rk,rj->kj', stack, stack, preferred_element_type=jnp...]
    another operation x24 -> x0, other arithmetic: 142 us -> none  [the longest x16 89.2 us: local(): lower = jnp.linalg.cholesky(gram)]
    pallas_call x0 -> x2, Pallas kernels: none -> 76 us  [the longest x1 55.2 us: reduced(): pl.pallas_call(reduce_kernel, out_shape=(jax.ShapeDtypeStruct((ROWS, B),...]
    ppermute x4 -> x0, starting transfers between devices: 24.8 us -> none  [the longest x2 17.2 us: padded(): lax.ppermute(lax.slice_in_dim(block, 0, width, axis=dim), axis, backward)]
    another operation x15 -> x0, matrix products: 24 us -> none  [the longest x8 17.8 us: local(): lax.linalg.triangular_solve(lower, stack.astype(jnp.float32), left_side=F...]
    another operation x30 -> x0, local copies, waits for them, and re-layouts: 19 us -> none
  transfers between devices with their start and end apart: 5 -> 0, of which waited for: 3 -> 0; matrix products, arithmetic and copies ran while one was open for 0% -> 0% of each run, Pallas kernels for 0% -> 0%
where the time goes in v1:
time: 80.4 us; the launch traced here: 80.2 us
  Pallas kernels  76 us (95%)
  local copies, waits for them, and re-layouts  3.53 us (4%)
    pallas_call x1, Pallas kernels, reduced(): pl.pallas_call(reduce_kernel, out_shape=(jax.ShapeDtypeStruct((ROWS, B),...  55.2 us
    pallas_call x1, Pallas kernels, k2(): pl.pallas_call(functools.partial(kern, total, nblk), out_shape=(jax.Shape...  20.8 us
    unnamed x8, local copies, waits for them, and re-layouts  2.94 us

profile of v1, /device:TPU:1, one launch (start us, length us, event | category | flops | bytes accessed | tf_op | source)
XLA Modules:
  0.0 80.2 jit_solution(4552160375178246175)
XLA Ops:
  0.6 0.0 copy-start
  0.6 1.1 %copy-done = bf16[3,1,2,128,512]{4,3,2,1,0:T(8,128)(2,1)S(1)} copy-done((bf16[3,1,2,128,512]{4,3,2,1,0:T(8,128)(2,1)S(1)}, bf16[3,1,2,128,512]{4,3,2,1,0:T(8,128)(2,1)}, u32[]{:S(2)}) %copy-start) | copy-done | bytes 786456
  1.8 0.0 copy-start.2
  1.8 1.1 %copy-done.2 = bf16[3,8,16,1024]{3,2,1,0:T(8,128)(2,1)S(1)} copy-done((bf16[3,8,16,1024]{3,2,1,0:T(8,128)(2,1)S(1)}, bf16[3,8,16,1024]{3,2,1,0:T(8,128)(2,1)}, u32[]{:S(2)}) %copy-start.2) | copy-done | bytes 786456
  2.9 0.0 copy-start.3
  2.9 0.7 copy-done.3
  3.6 0.0 copy-start.1
  3.6 55.2 %reduce.1 = (f32[1536,128]{1,0:T(8,128)S(1)}, f32[6,128]{1,0:T(8,128)S(1)}) custom-call(bf16[3,17]{1,0:T(4,128)(2,1)S(1)} %copy-done.3, bf16[384,1024]{1,0:T(8,128)(2,1)S(1)} %bitcast.8, bf16[768,512]{1,0:T(8,128)(2,1)S(1)} %bitcast.6), custom_call_target="tpu_custom_call" | custom-call | tf_op jit(solution)/shard_map/reduce/pallas_call | solution.py:319
  58.8 0.0 copy-done.1
  58.8 20.8 %factor.1 = (bf16[768,512]{1,0:T(8,128)(2,1)}, f32[6,128]{1,0:T(8,128)S(1)}, f32[513,513]{1,0:T(8,128)}) custom-call(f32[1536,128]{1,0:T(8,128)S(1)} %get-tuple-element.8.g_ref, f32[6,128]{1,0:T(8,128)S(1)} %get-tuple-element.9.f_ref, bf16[768,512]{1,0:T(8,128)(2,1)S(1)} %bitcast.7), custom_call_target="tpu_custom_call" | custom-call | tf_op jit(solution)/shard_map/factor/pallas_call | solution.py:134
  79.6 0.6 reshape.21
Async XLA Ops:
  0.6 1.1 %copy-start = (bf16[3,1,2,128,512]{4,3,2,1,0:T(8,128)(2,1)S(1)}, bf16[3,1,2,128,512]{4,3,2,1,0:T(8,128)(2,1)}, u32[]{:S(2)}) copy-start(bf16[3,1,2,128,512]{4,3,2,1,0:T(8,128)(2,1)} %param.4) | copy-start | bytes 2359300
  1.8 1.1 %copy-start.2 = (bf16[3,8,16,1024]{3,2,1,0:T(8,128)(2,1)S(1)}, bf16[3,8,16,1024]{3,2,1,0:T(8,128)(2,1)}, u32[]{:S(2)}) copy-start(bf16[3,8,16,1024]{3,2,1,0:T(8,128)(2,1)} %param.3) | copy-start | bytes 2359300
  2.9 0.7 copy-start.3
  3.6 55.3 %copy-start.1 = (bf16[3,1,2,128,512]{4,3,2,1,0:T(8,128)(2,1)S(1)}, bf16[3,1,2,128,512]{4,3,2,1,0:T(8,128)(2,1)}, u32[]{:S(2)}) copy-start(bf16[3,1,2,128,512]{4,3,2,1,0:T(8,128)(2,1)} %param.4) | copy-start | bytes 2359300

commit v2 on v1

v2 whole, which is shorter than its diff:
```python
import functools
import jax, jax.numpy as jnp
from jax import lax
from jax.sharding import PartitionSpec as P
from jax.experimental import pallas as pl
from jax.experimental.pallas import tpu as pltpu

F32, BF16 = jnp.float32, jnp.bfloat16
B = 128
HI = lax.Precision.HIGHEST

def lane_splat(tile, lane):
    return jnp.broadcast_to(tile[:, lane:lane + 1], (8, B))

def row_splat(tile, row):
    return jnp.broadcast_to(tile[row:row + 1, :], (8, B))

def recip(x):
    r = pl.reciprocal(x, approx=True)
    r = r * (2.0 - x * r)
    return r

def factor_block(a):
    sub = lax.broadcasted_iota(jnp.int32, (8, B), 0)
    lane = lax.broadcasted_iota(jnp.int32, (8, B), 1)
    n = B // 8
    a = list(a)
    z = [jnp.where(lane == 8 * t + sub, 1.0, 0.0) for t in range(n)]
    diag = [lane_splat(a[0], j) for j in range(8)]
    for p in range(n):
        cols = diag
        inv = []
        row = {}
        pivots = jnp.ones((8, B), F32)
        for k in range(8):
            pivot = row_splat(cols[k], k)
            pivots = jnp.where(sub == k, pivot, pivots)
            r = recip(pivot)
            inv.append(r)
            m = jnp.where(sub > k, cols[k] * r, 0.0)
            for j in range(k + 1, 8):
                row[k, j] = row_splat(cols[j], k)
                cols[j] = cols[j] - m * row[k, j]
            if k < 7:
                a[p] = a[p] - m * row_splat(a[p], k)
                z[p] = z[p] - m * row_splat(z[p], k)
        mult = {}
        for t in range(p + 1, n):
            c = [lane_splat(a[t], 8 * p + j) for j in range(8)]
            for k in range(8):
                m = c[k] * inv[k]
                mult[t, k] = m
                for j in range(k + 1, 8):
                    c[j] = c[j] - m * row[k, j]
            if t == p + 1:
                diag = []
                for j in range(8):
                    d = lane_splat(a[t], 8 * t + j)
                    for k in range(8):
                        d = d - mult[t, k] * row_splat(c[k], j)
                    diag.append(d)
        for k in range(8):
            if p + 1 < n:
                ua, uz = row_splat(a[p], k), row_splat(z[p], k)
            for t in range(p + 1, n):
                a[t] = a[t] - mult[t, k] * ua
                z[t] = z[t] - mult[t, k] * uz
        s = lax.rsqrt(pivots)
        a[p] = jnp.where(lane >= 8 * p + sub, a[p] * s, 0.0)
        z[p] = z[p] * s
    return a, z

PAIRS = [(b, c) for b in range(4) for c in range(b, 4)]
INDEX = {pair: i for i, pair in enumerate(PAIRS)}

def nn(x, y): return lax.dot_general(x, y, (((1,), (0,)), ((), ())), precision=HI, preferred_element_type=F32)
def tn(x, y): return lax.dot_general(x, y, (((0,), (0,)), ((), ())), precision=HI, preferred_element_type=F32)
def nt(x, y): return lax.dot_general(x, y, (((1,), (1,)), ((), ())), precision=HI, preferred_element_type=F32)
def nt16(x, y): return lax.dot_general(x, y, (((1,), (1,)), ((), ())), preferred_element_type=F32)

def split(x):
    hi = x.astype(BF16)
    return hi, (x - hi.astype(F32)).astype(BF16)

def k2_kernel(total, nblk, g_ref, col_ref, f_ref, basis_hbm, modes_ref, mode_ref, factor_ref, s_ref, zw_ref, zh_ref, zl_ref, basis_ref, load_s):
    load = pltpu.make_async_copy(basis_hbm, basis_ref, load_s)
    load.start()
    scale = 1.0 / total
    for i in range(160):
        s_ref[i // 16, 8 * (i % 16):8 * (i % 16) + 8, :] = g_ref[i // 5, 8 * (i % 5):8 * (i % 5) + 8, :] * scale
    grow = [col_ref[i:i + 1, :] * scale for i in range(5)]
    factor_ref[...] = jnp.zeros_like(factor_ref)
    zh_ref[...] = jnp.zeros_like(zh_ref)
    zl_ref[...] = jnp.zeros_like(zl_ref)
    zw_ref[...] = jnp.zeros_like(zw_ref)
    for b in range(nblk):
        blk = INDEX[b, b]
        a, z = factor_block([s_ref[blk, 8 * t:8 * t + 8, :] for t in range(16)])
        w = jnp.concatenate(z, axis=0)
        lo = b * B
        factor_ref[lo:lo + B, lo:lo + B] = jnp.concatenate(a, axis=0)
        zw_ref[lo:lo + B, lo:lo + B] = w
        r = {}
        for c in range(b + 1, 4):
            r[c] = nn(w, s_ref[INDEX[b, c]])
            factor_ref[lo:lo + B, c * B:(c + 1) * B] = r[c]
        if b:
            zw_ref[lo:lo + B, 0:lo] = nn(w, zw_ref[lo:lo + B, 0:lo])
        zrow = zw_ref[lo:lo + B, 0:lo + B]
        for i in range(b + 1, 4):
            for c in range(i, 4):
                s_ref[INDEX[i, c]] = s_ref[INDEX[i, c]] - tn(r[i], r[c])
            zw_ref[i * B:(i + 1) * B, 0:lo + B] = zw_ref[i * B:(i + 1) * B, 0:lo + B] - tn(r[i], zrow)
        zh, zl = split(zrow)
        if b == 0:
            load.wait()
        zh_ref[lo:lo + B, 0:lo + B] = zh
        zl_ref[lo:lo + B, 0:lo + B] = zl
        out = nt16(basis_ref[:, 0:lo + B], zh_ref[lo:lo + B, 0:lo + B]) + nt16(basis_ref[:, 0:lo + B], zl_ref[lo:lo + B, 0:lo + B])
        modes_ref[:, lo:lo + B] = out.astype(BF16)
    g4 = jnp.concatenate(grow[:4], axis=1)
    g8 = jnp.broadcast_to(g4, (8, 512))
    zall = zw_ref[...]
    rcol = nt(zall, g8)
    rrow = nt(g8, zall)
    v = nn(rrow, zall)
    d2 = grow[4][:, 0:1] - jnp.sum(rrow[0:1] * rrow[0:1], axis=1, keepdims=True)
    inv_d = lax.rsqrt(d2)
    factor_ref[0:512, 512:513] = rcol[:, 0:1]
    factor_ref[512:513, 512:513] = d2 * inv_d
    vh, vl = split(v)
    y = nt16(vh, basis_ref[...]) + nt16(vl, basis_ref[...])
    y6 = jnp.concatenate([y[0:1, i * B:(i + 1) * B] for i in range(6)], axis=0)
    mode_ref[...] = (f_ref[...] - y6) * inv_d

def k2(g, col, f, basis, total=393216.0, nblk=4, kern=k2_kernel):
    rows = basis.shape[0]
    return pl.pallas_call(
        functools.partial(kern, total, nblk),
        out_shape=(jax.ShapeDtypeStruct((rows, 512), BF16), jax.ShapeDtypeStruct((6, B), F32), jax.ShapeDtypeStruct((513, 513), F32)),
        in_specs=[pl.BlockSpec(memory_space=pltpu.VMEM)] * 3 + [pl.BlockSpec(memory_space=pltpu.HBM)],
        out_specs=[pl.BlockSpec(memory_space=pltpu.VMEM)] * 3,
        scratch_shapes=[pltpu.VMEM((10, B, B), F32), pltpu.VMEM((512, 512), F32), pltpu.VMEM((512, 512), BF16), pltpu.VMEM((512, 512), BF16), pltpu.VMEM((768, 512), BF16), pltpu.SemaphoreType.DMA],
        compiler_params=pltpu.CompilerParams(vmem_limit_bytes=40 << 20),
        name="factor",
    )(g, col, f, basis)

MESH = pl.DeviceIdType.MESH
NPLANE, NZR, CH, CG = 16, 16, 48, 40
PIECE = CH // NZR
NEAR = [(dx, dy) for dx in (0, 1, -1) for dy in (0, 1, -1) if (dx, dy) != (0, 0)]
AROUND = sorted(((dx, dy) for dx in range(4) for dy in range(4) if dx or dy), key=lambda o: -(min(o[0], 4 - o[0]) + min(o[1], 4 - o[1])))
ALONG = sorted(range(1, NZR), key=lambda k: -min(k, NZR - k))


def tap_tiles(taps, d, sub):
    def at(i):
        return jnp.broadcast_to(taps[d:d + 1, i:i + 1], (8, B))
    ahead = behind = jnp.zeros((8, B), F32)
    for s in range(8):
        ahead = jnp.where(sub == s, at(8 + s), ahead)
        behind = jnp.where(sub == s, at(s), behind)
    return ahead, behind, jnp.where(sub == 0, at(16), 0.0)


def reduce_kernel(taps_hbm, snap_hbm, basis_hbm, full_ref, col_ref, filt_ref, taps_ref, snap_ref, basis_ref, band_ref, near_out, near_in, acc, recv_a, recv_b, chunk_ref, recv_c, piece_ref, ring_ref, whole_ref, gsend, grecv, gsib, gin, gout, gz, load_s, near_s, near_r, sa, ra, sb, rb, sc, rc, sd, rd, se, re, sf, rf, sga, rga, sgb, rgb, sgc, rgc, far):
    gx, gy = lax.axis_index("gx"), lax.axis_index("gy")
    x, z = gx // NZR, gx % NZR
    y, core = gy // 2, gy % 2
    plane = x * 4 + y

    def near_id(dx, dy):
        return ((gx + dx + 64) % 64, (gy + dy + 8) % 8)

    def plane_at(o):
        return ((x + o[0]) % 4) * 4 + (y + o[1]) % 4

    def plane_id(o):
        return (((x + o[0]) % 4) * NZR + z, ((y + o[1]) % 4) * 2 + core)

    def z_id(k):
        return (x * NZR + (z + k) % NZR, gy)

    sibling = (gx, y * 2 + (1 - core))
    barrier = pltpu.get_barrier_semaphore()
    partners = [near_id(dx, dy) for dx, dy in NEAR] + [plane_id(o) for o in AROUND] + [z_id(k) for k in ALONG if min(k, NZR - k) <= 4] + [sibling]
    for partner in partners:
        pl.semaphore_signal(barrier, inc=1, device_id=partner, device_id_type=MESH)
    loads = []
    for i in range(3):
        loads.append(pltpu.make_async_copy(basis_hbm.at[pl.ds(256 * i, 256)], basis_ref.at[pl.ds(256 * i, 256)], load_s.at[4 + i]))
    loads.append(pltpu.make_async_copy(taps_hbm, taps_ref, load_s.at[0]))
    for i in range(3):
        loads.append(pltpu.make_async_copy(snap_hbm.at[pl.ds(128 * i, 128)], snap_ref.at[pl.ds(128 * i, 128)], load_s.at[1 + i]))
    for c in loads:
        c.start()

    sub = lax.broadcasted_iota(jnp.int32, (8, B), 0)
    lane = lax.broadcasted_iota(jnp.int32, (8, B), 1)
    for c in loads[:3]:
        c.wait()
    at = 0
    for b in range(4):
        part = lax.dot_general(basis_ref[:, b * B:(b + 1) * B], basis_ref[:, b * B:512], (((0,), (0,)), ((), ())), preferred_element_type=F32)
        for c in range(4 - b):
            acc[at:at + B, :] = part[:, c * B:(c + 1) * B]
            at += B
    pl.semaphore_wait(barrier, len(partners))
    for k in (4, NZR - 4):
        pl.semaphore_signal(far, inc=1, device_id=z_id(k), device_id_type=MESH)

    def copy(src, dst, ssem, rsem, device):
        c = pltpu.make_async_remote_copy(src_ref=src, dst_ref=dst, send_sem=ssem, recv_sem=rsem, device_id=device, device_id_type=MESH)
        c.start()
        return c

    half = NPLANE * CG
    ca = copy(acc.at[pl.ds((1 - core) * half, half)], recv_a, sa, ra, sibling)
    loads[3].wait()
    taps = taps_ref[...].astype(F32)
    ahead, behind, last = tap_tiles(taps, 2, sub)
    for m in range(0, 128, 2):
        pair = []
        for t in (m, m + 1):
            tile = jnp.where(lane == t, ahead, 0.0)
            tile = jnp.where(lane == (t + 1) % 128, behind, tile)
            pair.append(jnp.where(lane == (t + 127) % 128, last, tile))
        band_ref[8 * m:8 * m + 16, :] = jnp.concatenate(pair, axis=0).astype(BF16)
    for c in loads[4:]:
        c.wait()
    along_z = jnp.dot(snap_ref[...], band_ref[...], preferred_element_type=F32)
    ahead, behind, last = tap_tiles(taps, 0, sub)
    w_ahead = [row_splat(ahead, s) for s in range(8)]
    w_behind = [row_splat(behind, s) for s in range(8)]
    w_last = row_splat(last, 0)
    ahead, behind, last = tap_tiles(taps, 1, sub)
    sums = {}
    for dx in (0, 1, -1):
        for dy in (0, 1, -1):
            sums[dx, dy] = jnp.zeros((8, B), F32)
    for c in range(3):
        cell = [[along_z[(c * 8 + i) * 16 + 8 * h:(c * 8 + i) * 16 + 8 * h + 8, :] for i in range(8)] for h in range(2)]
        for dx in (0, 1, -1):
            part = []
            for h in range(2):
                if dx == -1:
                    part.append(w_last * cell[h][0])
                else:
                    w = w_ahead if dx == 0 else w_behind
                    v = w[0] * cell[h][0]
                    for i in range(1, 8):
                        v = v + w[i] * cell[h][i]
                    part.append(v)
            def put(dy, q, tile):
                total = jnp.sum(tile, axis=0, keepdims=True)
                sums[dx, dy] = jnp.where(sub == 2 * c + q, jnp.broadcast_to(total, (8, B)), sums[dx, dy])
            put(0, 0, ahead * part[0] + last * part[1])
            put(0, 1, behind * part[0] + ahead * part[1])
            put(1, 0, behind * part[1])
            put(-1, 1, last * part[0])
    for e, (dx, dy) in enumerate(NEAR):
        tile = sums[dx, dy]
        if dy == 1:
            tile = jnp.where(gy == 7, 0.0, tile)
        if dy == -1:
            tile = jnp.where(gy == 0, 0.0, tile)
        near_out[e] = tile
    near = [copy(near_out.at[e], near_in.at[e], near_s.at[e], near_r.at[e], near_id(dx, dy)) for e, (dx, dy) in enumerate(NEAR)]
    ca.wait_recv()
    def halved(p):
        rows = pl.ds(p * CG, CG)
        recv_a[rows, :] = recv_a[rows, :] + acc[pl.ds(core * half + p * CG, CG), :]
    cb = []
    for e, o in enumerate(AROUND):
        p = plane_at(o)
        halved(p)
        cb.append(copy(recv_a.at[pl.ds(p * CG, CG)], recv_b.at[e], sb.at[e], rb.at[e], plane_id(o)))
    halved(plane)
    total = recv_a[pl.ds(plane * CG, CG), :]
    for e in reversed(range(NPLANE - 1)):
        cb[e].wait_recv()
        total = total + recv_b[e]
    pl.semaphore_wait(far, 2)
    total = jnp.concatenate([total, jnp.zeros((CH - CG, B), F32)], axis=0)
    for i in range(NZR):
        chunk_ref[i] = total[i * PIECE:(i + 1) * PIECE, :]
    cc = []
    for e, k in enumerate(ALONG):
        cc.append(copy(chunk_ref.at[(z + k) % NZR], recv_c.at[e], sc.at[e], rc.at[e], z_id(k)))
    for c in near:
        c.wait_recv()
    f = sums[0, 0]
    for e in range(len(NEAR)):
        f = f + near_in[e]
    f16 = f.astype(BF16)
    f = f16.astype(F32)
    filt_ref[...] = f[0:6, :]
    frow = jnp.concatenate([jnp.broadcast_to(f[i:i + 1, :], (8, B)) for i in range(6)], axis=1).astype(BF16)
    g = jnp.dot(frow, basis_ref[...], preferred_element_type=F32)
    sq = jnp.where(sub < 6, f * f, 0.0)
    ff = jnp.sum(jnp.sum(sq, axis=1, keepdims=True), axis=0, keepdims=True)
    tail = jnp.where(sub == 4, jnp.broadcast_to(ff, (8, B)), 0.0)
    for i in range(4):
        tail = jnp.where(sub == i, g[:, i * B:(i + 1) * B], tail)
    gsend[...] = tail
    cga = copy(gsend, gsib, sga, rga, sibling)
    cga.wait_recv()
    gin[plane] = tail + gsib[...]
    cgb = [copy(gin.at[plane], gin.at[plane], sgb.at[e], rgb.at[e], plane_id(o)) for e, o in enumerate(AROUND)]
    total = chunk_ref[z]
    for e in reversed(range(NZR - 1)):
        cc[e].wait_recv()
        total = total + recv_c[e]
    piece_ref[...] = total
    cd = []
    for e, k in enumerate(ALONG):
        cd.append(copy(piece_ref, ring_ref.at[z], sd.at[e], rd.at[e], z_id(k)))
    ring_ref[z] = total
    for c in reversed(cgb):
        c.wait_recv()
    column = gin[0]
    for i in range(1, NPLANE):
        column = column + gin[i]
    gout[...] = column
    gz[z] = column
    cgc = [copy(gout, gz.at[z], sgc.at[e], rgc.at[e], z_id(k)) for e, k in enumerate(ALONG)]
    for c in reversed(cd):
        c.wait_recv()
    for i in range(NZR):
        whole_ref[i * PIECE:(i + 1) * PIECE, :] = ring_ref[i]
    rows = pl.ds(0, CG)
    def slot(c, p):
        return full_ref.at[c * NPLANE + p, rows]
    ce = []
    for e, o in enumerate(AROUND):
        ce.append(copy(whole_ref.at[rows], slot(core, plane), se.at[e], re.at[e], plane_id(o)))
    cf = [copy(whole_ref.at[rows], slot(core, plane), sf.at[NPLANE - 1], rf.at[NPLANE - 1], sibling)]
    full_ref[core * NPLANE + plane] = whole_ref[0:CG, :]
    for e in reversed(range(NPLANE - 1)):
        ce[e].wait_recv()
        p = plane_at((4 - AROUND[e][0], 4 - AROUND[e][1]))
        cf.append(copy(slot(core, p), slot(core, p), sf.at[e], rf.at[e], sibling))
    for c in reversed(cgc):
        c.wait_recv()
    column = gz[0]
    for i in range(1, NZR):
        column = column + gz[i]
    col_ref[...] = column
    for c in cf:
        c.wait_recv()
    for c in near + [ca, cga] + cb + cgb + cc + cd + cgc + ce + cf:
        c.wait_send()


def reduced(taps, snap, basis):
    dma = pltpu.SemaphoreType.DMA
    vmem = pltpu.VMEM
    n = NPLANE - 1
    return pl.pallas_call(
        reduce_kernel,
        out_shape=(jax.ShapeDtypeStruct((2 * NPLANE, CG, B), F32), jax.ShapeDtypeStruct((8, B), F32), jax.ShapeDtypeStruct((6, B), F32)),
        in_specs=[pl.BlockSpec(memory_space=pltpu.HBM)] * 3,
        out_specs=[pl.BlockSpec(memory_space=vmem)] * 3,
        scratch_shapes=[
            vmem((3, 17), BF16),
            vmem((384, 1024), BF16),
            vmem((768, 512), BF16),
            vmem((1024, B), BF16),
            vmem((8, 8, B), F32),
            vmem((8, 8, B), F32),
            vmem((2 * NPLANE * CG, B), F32),
            vmem((NPLANE * CG, B), F32),
            vmem((n, CG, B), F32),
            vmem((NZR, PIECE, B), F32),
            vmem((n, PIECE, B), F32),
            vmem((PIECE, B), F32),
            vmem((NZR, PIECE, B), F32),
            vmem((CH, B), F32),
            vmem((8, B), F32),
            vmem((8, B), F32),
            vmem((8, B), F32),
            vmem((NPLANE, 8, B), F32),
            vmem((8, B), F32),
            vmem((NZR, 8, B), F32),
            dma((7,)), dma((8,)), dma((8,)), dma, dma,
            dma((n,)), dma((n,)), dma((n,)), dma((n,)), dma((n,)), dma((n,)), dma((n,)), dma((n,)), dma((n + 1,)), dma((n + 1,)),
            dma, dma, dma((n,)), dma((n,)), dma((n,)), dma((n,)), pltpu.SemaphoreType.REGULAR,
        ],
        compiler_params=pltpu.CompilerParams(vmem_limit_bytes=40<<20, collective_id=0, has_side_effects=True),
        name="reduce",
    )(*(pltpu.with_memory_space_constraint(v, pltpu.HBM) for v in (taps, snap, basis)))


def local(snapshot, basis, taps):
    flat = basis.reshape(-1, basis.shape[-1])
    g, col, f = reduced(taps, snapshot.reshape(-1, snapshot.shape[-1]), flat)
    total = flat.shape[0] * lax.axis_size("gx") * lax.axis_size("gy")
    modes, mode, fac = k2(g, col, f, flat, float(total))
    return modes.reshape(basis.shape), mode.reshape(basis.shape[:-1]), fac


def solution(mesh):
    in_specs = (P(None, "gx", "gy", None), P(None, "gx", "gy", None, None), P())
    out_specs = (P(None, "gx", "gy", None, None), P(None, "gx", "gy", None), P())
    return jax.shard_map(local, mesh=mesh, in_specs=in_specs, out_specs=out_specs, check_vma=False)
```

time: 80.4 us -> 68.7 us (0.85)
  Pallas kernels: 76 us -> 67.4 us
  local copies, waits for them, and re-layouts: 3.53 us -> 0.59 us
    pallas_call x1, Pallas kernels: 55.2 us -> 45.9 us  [reduced(): pl.pallas_call(reduce_kernel, out_shape=(jax.ShapeDtypeStruct((2 * NPLANE...]
    unnamed x8 -> x2, local copies, waits for them, and re-layouts: 2.94 us -> 0.01 us
where the time goes in v2:
time: 68.7 us; the launch traced here: 68.6 us
  Pallas kernels  67.4 us (98%)
    pallas_call x1, Pallas kernels, reduced(): pl.pallas_call(reduce_kernel, out_shape=(jax.ShapeDtypeStruct((2 * NPLANE...  45.9 us
    pallas_call x1, Pallas kernels, k2(): pl.pallas_call(functools.partial(kern, total, nblk), out_shape=(jax.Shape...  21.4 us

profile of v2, /device:TPU:1, one launch (start us, length us, event | category | flops | bytes accessed | tf_op | source)
XLA Modules:
  0.0 68.6 jit_solution(15421639198364734531)
XLA Ops:
  0.6 0.0 copy-start
  0.6 45.9 %reduce.1 = (f32[32,40,128]{2,1,0:T(8,128)S(1)}, f32[8,128]{1,0:T(8,128)S(1)}, f32[6,128]{1,0:T(8,128)S(1)}) custom-call(bf16[3,17]{1,0:T(4,128)(2,1)} %taps_hbm.1, bf16[384,1024]{1,0:T(8,128)(2,1)} %bitcast.8, bf16[768,512]{1,0:T(8,128)(2,1)} %bitcast.6), custom_call_target="tpu_custom_call" | custom-call | tf_op jit(solution)/shard_map/reduce/pallas_call | solution.py:359
  46.6 0.0 copy-done
  46.6 21.4 %factor.1 = (bf16[768,512]{1,0:T(8,128)(2,1)}, f32[6,128]{1,0:T(8,128)S(1)}, f32[513,513]{1,0:T(8,128)}) custom-call(f32[32,40,128]{2,1,0:T(8,128)S(1)} %get-tuple-element.9.g_ref, f32[8,128]{1,0:T(8,128)S(1)} %get-tuple-element.10.col_ref, f32[6,128]{1,0:T(8,128)S(1)} %get-tuple-element.11.f_ref, bf16[768,512]{1,0:T(8,128)(2,1)S(1)} %bitcast.7), custom_call_target="tpu_custom_call" | custom-call | tf_op jit(solution)/shard_map/factor/pallas_call | solution.py:138
  68.0 0.6 reshape.21
Async XLA Ops:
  0.6 45.9 %copy-start = (bf16[3,1,2,128,512]{4,3,2,1,0:T(8,128)(2,1)S(1)}, bf16[3,1,2,128,512]{4,3,2,1,0:T(8,128)(2,1)}, u32[]{:S(2)}) copy-start(bf16[3,1,2,128,512]{4,3,2,1,0:T(8,128)(2,1)} %param.4) | copy-start | bytes 2359300

commit v3 on v2

--- a/solution.py
+++ b/solution.py
@@ -6,141 +6,223 @@
 from jax.experimental.pallas import tpu as pltpu
 
 F32, BF16 = jnp.float32, jnp.bfloat16
-B = 128
+B, H = 128, 64
 HI = lax.Precision.HIGHEST
 
+
 def lane_splat(tile, lane):
-    return jnp.broadcast_to(tile[:, lane:lane + 1], (8, B))
+    return jnp.take_along_axis(tile, jnp.full((8, B), lane, jnp.int32), axis=1)
+
 
 def row_splat(tile, row):
     return jnp.broadcast_to(tile[row:row + 1, :], (8, B))
 
-def recip(x):
-    r = pl.reciprocal(x, approx=True)
-    r = r * (2.0 - x * r)
-    return r
-
-def factor_block(a):
-    sub = lax.broadcasted_iota(jnp.int32, (8, B), 0)
-    lane = lax.broadcasted_iota(jnp.int32, (8, B), 1)
-    n = B // 8
-    a = list(a)
-    z = [jnp.where(lane == 8 * t + sub, 1.0, 0.0) for t in range(n)]
-    diag = [lane_splat(a[0], j) for j in range(8)]
-    for p in range(n):
-        cols = diag
-        inv = []
-        row = {}
-        pivots = jnp.ones((8, B), F32)
-        for k in range(8):
-            pivot = row_splat(cols[k], k)
-            pivots = jnp.where(sub == k, pivot, pivots)
-            r = recip(pivot)
-            inv.append(r)
-            m = jnp.where(sub > k, cols[k] * r, 0.0)
-            for j in range(k + 1, 8):
-                row[k, j] = row_splat(cols[j], k)
-                cols[j] = cols[j] - m * row[k, j]
-            if k < 7:
-                a[p] = a[p] - m * row_splat(a[p], k)
-                z[p] = z[p] - m * row_splat(z[p], k)
-        mult = {}
-        for t in range(p + 1, n):
-            c = [lane_splat(a[t], 8 * p + j) for j in range(8)]
-            for k in range(8):
-                m = c[k] * inv[k]
-                mult[t, k] = m
-                for j in range(k + 1, 8):
-                    c[j] = c[j] - m * row[k, j]
-            if t == p + 1:
-                diag = []
-                for j in range(8):
-                    d = lane_splat(a[t], 8 * t + j)
-                    for k in range(8):
-                        d = d - mult[t, k] * row_splat(c[k], j)
-                    diag.append(d)
-        for k in range(8):
-            if p + 1 < n:
-                ua, uz = row_splat(a[p], k), row_splat(z[p], k)
-            for t in range(p + 1, n):
-                a[t] = a[t] - mult[t, k] * ua
-                z[t] = z[t] - mult[t, k] * uz
-        s = lax.rsqrt(pivots)
-        a[p] = jnp.where(lane >= 8 * p + sub, a[p] * s, 0.0)
-        z[p] = z[p] * s
-    return a, z
-
-PAIRS = [(b, c) for b in range(4) for c in range(b, 4)]
-INDEX = {pair: i for i, pair in enumerate(PAIRS)}
-
-def nn(x, y): return lax.dot_general(x, y, (((1,), (0,)), ((), ())), precision=HI, preferred_element_type=F32)
-def tn(x, y): return lax.dot_general(x, y, (((0,), (0,)), ((), ())), precision=HI, preferred_element_type=F32)
-def nt(x, y): return lax.dot_general(x, y, (((1,), (1,)), ((), ())), precision=HI, preferred_element_type=F32)
-def nt16(x, y): return lax.dot_general(x, y, (((1,), (1,)), ((), ())), preferred_element_type=F32)
+
+def nn(x, y):
+    return lax.dot_general(x, y, (((1,), (0,)), ((), ())), precision=HI, preferred_element_type=F32)
+
+
+def tn(x, y):
+    return lax.dot_general(x, y, (((0,), (0,)), ((), ())), precision=HI, preferred_element_type=F32)
+
+
+def nt(x, y):
+    return lax.dot_general(x, y, (((1,), (1,)), ((), ())), precision=HI, preferred_element_type=F32)
+
+
+def nt16(x, y):
+    return lax.dot_general(x, y, (((1,), (1,)), ((), ())), preferred_element_type=F32)
+
 
 def split(x):
     hi = x.astype(BF16)
     return hi, (x - hi.astype(F32)).astype(BF16)
 
-def k2_kernel(total, nblk, g_ref, col_ref, f_ref, basis_hbm, modes_ref, mode_ref, factor_ref, s_ref, zw_ref, zh_ref, zl_ref, basis_ref, load_s):
+
+def factor_half(a, off, tick):
+    sub = lax.broadcasted_iota(jnp.int32, (8, B), 0)
+    lane = lax.broadcasted_iota(jnp.int32, (8, B), 1)
+    mine = (lane >= H) if off else (lane < H)
+    n = H // 8
+    a = [jnp.where(mine, a[t], jnp.where(lane + off - H == 8 * t + sub, 1.0, 0.0)) for t in range(n)]
+    diag = [lane_splat(a[0], off + j) for j in range(8)]
+    for p in range(n):
+        cols = diag
+        below = range(p + 1, n)
+        c = {t: [lane_splat(a[t], off + 8 * p + j) for j in range(8)] for t in below}
+        if below:
+            diag = [lane_splat(a[p + 1], off + 8 * (p + 1) + j) for j in range(8)]
+        inv, row, mult = [], {}, {}
+        pivots = jnp.ones((8, B), F32)
+        pivot = row_splat(cols[0], 0)
+        for k in range(8):
+            pivots = jnp.where(sub == k, pivot, pivots)
+            r = pl.reciprocal(pivot, approx=True)
+            inv.append(r)
+            m = cols[k] * r
+            for j in range(k + 1, 8):
+                row[k, j] = row_splat(cols[j], k)
+            if k < 7:
+                pivot = row_splat(cols[k + 1], k + 1) - (row[k, k + 1] * row[k, k + 1]) * r
+                for j in range(k + 1, 8):
+                    cols[j] = cols[j] - m * row[k, j]
+                a[p] = a[p] - jnp.where(sub > k, m, 0.0) * row_splat(a[p], k)
+        for t in below:
+            for k in range(8):
+                mult[t, k] = c[t][k] * inv[k]
+                for j in range(k + 1, 8):
+                    c[t][j] = c[t][j] - mult[t, k] * row[k, j]
+        if below:
+            for j in range(8):
+                for k in range(8):
+                    diag[j] = diag[j] - mult[p + 1, k] * row_splat(c[p + 1][k], j)
+            for k in range(8):
+                u = row_splat(a[p], k)
+                for t in below:
+                    a[t] = a[t] - mult[t, k] * u
+        a[p] = a[p] * lax.rsqrt(pivots)
+        tick()
+    return jnp.concatenate(a, axis=0)
+
+
+def factor_block(x, tick):
+    lane = lax.broadcasted_iota(jnp.int32, (H, B), 1)
+    rows = lax.broadcasted_iota(jnp.int32, (H, B), 0)
+    low = lane < H
+    zero = jnp.zeros((H, B), F32)
+    p0 = factor_half([x[8 * t:8 * t + 8] for t in range(8)], 0, tick)
+    r01 = nn(p0, jnp.concatenate([zero, jnp.where(low, 0.0, x[0:H])], axis=0))
+    s11 = x[H:B] - tn(r01, r01)[H:B]
+    w0 = jnp.where(low, pltpu.roll(p0, H, 1), 0.0)
+    t10 = tn(r01, w0)[H:B]
+    p1 = factor_half([s11[8 * t:8 * t + 8] for t in range(8)], H, tick)
+    w10 = nn(p1, jnp.concatenate([t10, zero], axis=0))
+    r = jnp.concatenate([jnp.where(low, jnp.where(lane >= rows, p0, 0.0), r01), jnp.where(lane >= rows + H, p1, 0.0)], axis=0)
+    w = jnp.concatenate([w0, jnp.where(low, -w10, pltpu.roll(p1, H, 1))], axis=0)
+    return r, w
+
+
+PAIRS = [(b, c) for b in range(4) for c in range(b, 4)]
+INDEX = {pair: i for i, pair in enumerate(PAIRS)}
+
+
+def k2_kernel(total, g_ref, col_ref, f_ref, basis_hbm, modes_hbm, mode_ref, factor_hbm, s_ref, zw_ref, zh_ref, zl_ref, basis_ref, modes_ref, factor_ref, load_s, out_s, fac_s):
     load = pltpu.make_async_copy(basis_hbm, basis_ref, load_s)
     load.start()
     scale = 1.0 / total
     for i in range(160):
         s_ref[i // 16, 8 * (i % 16):8 * (i % 16) + 8, :] = g_ref[i // 5, 8 * (i % 5):8 * (i % 5) + 8, :] * scale
-    grow = [col_ref[i:i + 1, :] * scale for i in range(5)]
+    col = col_ref[...] * scale
+    g8 = jnp.broadcast_to(jnp.concatenate([col[i:i + 1, :] for i in range(4)], axis=1), (8, 512))
     factor_ref[...] = jnp.zeros_like(factor_ref)
+    zw_ref[...] = jnp.zeros_like(zw_ref)
     zh_ref[...] = jnp.zeros_like(zh_ref)
     zl_ref[...] = jnp.zeros_like(zl_ref)
-    zw_ref[...] = jnp.zeros_like(zw_ref)
-    for b in range(nblk):
-        blk = INDEX[b, b]
-        a, z = factor_block([s_ref[blk, 8 * t:8 * t + 8, :] for t in range(16)])
-        w = jnp.concatenate(z, axis=0)
-        lo = b * B
-        factor_ref[lo:lo + B, lo:lo + B] = jnp.concatenate(a, axis=0)
-        zw_ref[lo:lo + B, lo:lo + B] = w
-        r = {}
-        for c in range(b + 1, 4):
-            r[c] = nn(w, s_ref[INDEX[b, c]])
-            factor_ref[lo:lo + B, c * B:(c + 1) * B] = r[c]
+    outs = []
+    later = []
+    state = [jnp.zeros((8, 512), F32), jnp.zeros((8, 1), F32)]
+
+    def tick():
+        if later:
+            later.pop(0)()
+
+    def start(src, dst, sem):
+        outs.append(pltpu.make_async_copy(src, dst, sem))
+        outs[-1].start()
+
+    def panel(b, c):
+        return factor_ref[b * B:(b + 1) * B, c * B:(c + 1) * B]
+
+    def factor_off(b, c, w):
+        factor_ref[b * B:(b + 1) * B, c * B:(c + 1) * B] = nn(w, s_ref[INDEX[b, c]])
+
+    def inverse_row(b, w):
+        lo, hi = b * B, (b + 1) * B
         if b:
-            zw_ref[lo:lo + B, 0:lo] = nn(w, zw_ref[lo:lo + B, 0:lo])
-        zrow = zw_ref[lo:lo + B, 0:lo + B]
+            zw_ref[lo:hi, 0:lo] = nn(w, zw_ref[lo:hi, 0:lo])
+        zw_ref[lo:hi, lo:hi] = w
+        zh_ref[lo:hi, 0:hi], zl_ref[lo:hi, 0:hi] = split(zw_ref[lo:hi, 0:hi])
+
+    def trail(b, i, c):
+        s_ref[INDEX[i, c]] = s_ref[INDEX[i, c]] - tn(panel(b, i), panel(b, c))
+
+    def inverse_trail(b, i):
+        hi = (b + 1) * B
+        zw_ref[i * B:(i + 1) * B, 0:hi] = zw_ref[i * B:(i + 1) * B, 0:hi] - tn(panel(b, i), zw_ref[b * B:hi, 0:hi])
+
+    def column(b):
+        lo, hi = b * B, (b + 1) * B
+        zrow = zw_ref[lo:hi, :]
+        factor_ref[lo:hi, 512:513] = nt(zrow, g8)[:, 0:1]
+        start(factor_ref.at[pl.ds(lo, B)], factor_hbm.at[pl.ds(lo, B)], fac_s.at[b])
+        rrow = nt(g8, zrow)
+        state[1] = state[1] + jnp.sum(rrow * rrow, axis=1, keepdims=True)
+        state[0] = state[0] + nn(rrow, zrow)
+
+    def apply(b, part):
+        lo, hi = b * B, (b + 1) * B
+        if b == 0 and part == 0:
+            load.wait()
+        top = part * (rows // 2)
+        own = basis_ref[top:top + rows // 2, 0:hi]
+        out = nt16(own, zh_ref[lo:hi, 0:hi]) + nt16(own, zl_ref[lo:hi, 0:hi])
+        modes_ref[top:top + rows // 2, lo:hi] = out.astype(BF16)
+        at = (pl.ds(top, rows // 2), pl.ds(lo, B))
+        start(modes_ref.at[at], modes_hbm.at[at], out_s.at[2 * b + part])
+
+    rows = basis_ref.shape[0]
+    for b in range(4):
+        lo, hi = b * B, (b + 1) * B
+        r_own, w = factor_block(s_ref[INDEX[b, b]], tick)
+        while later:
+            tick()
+        if b < 3:
+            factor_off(b, b + 1, w)
+            trail(b, b + 1, b + 1)
+        factor_ref[lo:hi, lo:hi] = r_own
+        for c in range(b + 2, 4):
+            later.append(functools.partial(factor_off, b, c, w))
+        later.append(functools.partial(inverse_row, b, w))
         for i in range(b + 1, 4):
             for c in range(i, 4):
-                s_ref[INDEX[i, c]] = s_ref[INDEX[i, c]] - tn(r[i], r[c])
-            zw_ref[i * B:(i + 1) * B, 0:lo + B] = zw_ref[i * B:(i + 1) * B, 0:lo + B] - tn(r[i], zrow)
-        zh, zl = split(zrow)
-        if b == 0:
-            load.wait()
-        zh_ref[lo:lo + B, 0:lo + B] = zh
-        zl_ref[lo:lo + B, 0:lo + B] = zl
-        out = nt16(basis_ref[:, 0:lo + B], zh_ref[lo:lo + B, 0:lo + B]) + nt16(basis_ref[:, 0:lo + B], zl_ref[lo:lo + B, 0:lo + B])
-        modes_ref[:, lo:lo + B] = out.astype(BF16)
-    g4 = jnp.concatenate(grow[:4], axis=1)
-    g8 = jnp.broadcast_to(g4, (8, 512))
-    zall = zw_ref[...]
-    rcol = nt(zall, g8)
-    rrow = nt(g8, zall)
-    v = nn(rrow, zall)
-    d2 = grow[4][:, 0:1] - jnp.sum(rrow[0:1] * rrow[0:1], axis=1, keepdims=True)
+                if (i, c) != (b + 1, b + 1):
+                    later.append(functools.partial(trail, b, i, c))
+            later.append(functools.partial(inverse_trail, b, i))
+        if b < 3:
+            later.append(functools.partial(column, b))
+        later.append(functools.partial(apply, b, 0))
+        later.append(functools.partial(apply, b, 1))
+        if b == 3:
+            later.append(functools.partial(column, b))
+    while later:
+        tick()
+    v, norm = state
+    d2 = col[4:5, 0:1] - norm[0:1]
     inv_d = lax.rsqrt(d2)
-    factor_ref[0:512, 512:513] = rcol[:, 0:1]
     factor_ref[512:513, 512:513] = d2 * inv_d
+    outs.append(pltpu.make_async_copy(factor_ref.at[pl.ds(512, 1)], factor_hbm.at[pl.ds(512, 1)], fac_s.at[4]))
+    outs[-1].start()
     vh, vl = split(v)
     y = nt16(vh, basis_ref[...]) + nt16(vl, basis_ref[...])
-    y6 = jnp.concatenate([y[0:1, i * B:(i + 1) * B] for i in range(6)], axis=0)
-    mode_ref[...] = (f_ref[...] - y6) * inv_d
-
-def k2(g, col, f, basis, total=393216.0, nblk=4, kern=k2_kernel):
+    f = f_ref[...]
+    for i in range(6):
+        mode_ref[i // 2, i % 2:i % 2 + 1, :] = (f[i:i + 1, :] - y[0:1, i * B:(i + 1) * B]) * inv_d
+    for c in outs:
+        c.wait()
+
+
+def k2(g, col, f, basis, total):
     rows = basis.shape[0]
+    vmem, hbm, dma = pltpu.VMEM, pltpu.HBM, pltpu.SemaphoreType.DMA
     return pl.pallas_call(
-        functools.partial(kern, total, nblk),
-        out_shape=(jax.ShapeDtypeStruct((rows, 512), BF16), jax.ShapeDtypeStruct((6, B), F32), jax.ShapeDtypeStruct((513, 513), F32)),
-        in_specs=[pl.BlockSpec(memory_space=pltpu.VMEM)] * 3 + [pl.BlockSpec(memory_space=pltpu.HBM)],
-        out_specs=[pl.BlockSpec(memory_space=pltpu.VMEM)] * 3,
-        scratch_shapes=[pltpu.VMEM((10, B, B), F32), pltpu.VMEM((512, 512), F32), pltpu.VMEM((512, 512), BF16), pltpu.VMEM((512, 512), BF16), pltpu.VMEM((768, 512), BF16), pltpu.SemaphoreType.DMA],
+        functools.partial(k2_kernel, total),
+        out_shape=(jax.ShapeDtypeStruct((rows, 512), BF16), jax.ShapeDtypeStruct((3, 2, B), F32), jax.ShapeDtypeStruct((513, 513), F32)),
+        in_specs=[pl.BlockSpec(memory_space=vmem)] * 3 + [pl.BlockSpec(memory_space=hbm)],
+        out_specs=[pl.BlockSpec(memory_space=hbm), pl.BlockSpec(memory_space=vmem), pl.BlockSpec(memory_space=hbm)],
+        scratch_shapes=[
+            vmem((10, B, B), F32), vmem((512, 512), F32), vmem((512, 512), BF16), vmem((512, 512), BF16),
+            vmem((rows, 512), BF16), vmem((rows, 512), BF16), vmem((513, 513), F32), dma, dma((8,)), dma((5,)),
+        ],
         compiler_params=pltpu.CompilerParams(vmem_limit_bytes=40 << 20),
         name="factor",
     )(g, col, f, basis)

time: 68.7 us -> 62.2 us (0.905)
  Pallas kernels: 67.4 us -> 61.3 us
    pallas_call x1, Pallas kernels: 21.4 us -> 15.3 us  [k2(): pl.pallas_call(functools.partial(k2_kernel, total), out_shape=(jax.ShapeD...]
where the time goes in v3:
time: 62.2 us; the launch traced here: 62.1 us
  Pallas kernels  61.3 us (99%)
  between operations  0.81 us (1%)
    pallas_call x1, Pallas kernels, reduced(): pl.pallas_call(reduce_kernel, out_shape=(jax.ShapeDtypeStruct((2 * NPLANE...  45.9 us
    pallas_call x1, Pallas kernels, k2(): pl.pallas_call(functools.partial(k2_kernel, total), out_shape=(jax.ShapeD...  15.3 us

profile of v3, /device:TPU:1, one launch (start us, length us, event | category | flops | bytes accessed | tf_op | source)
XLA Modules:
  0.0 62.1 jit_solution(2001146427259383296)
XLA Ops:
  0.6 0.0 copy-start
  0.6 45.9 %reduce.1 = (f32[32,40,128]{2,1,0:T(8,128)S(1)}, f32[8,128]{1,0:T(8,128)S(1)}, f32[6,128]{1,0:T(8,128)S(1)}) custom-call(bf16[3,17]{1,0:T(4,128)(2,1)} %taps_hbm.1, bf16[384,1024]{1,0:T(8,128)(2,1)} %bitcast.10, bf16[768,512]{1,0:T(8,128)(2,1)} %bitcast.8), custom_call_target="tpu_custom_call" | custom-call | tf_op jit(solution)/shard_map/reduce/pallas_call | solution.py:441
  46.6 0.0 copy-done
  46.6 15.3 %factor.1 = (bf16[768,512]{1,0:T(8,128)(2,1)}, f32[3,2,128]{2,1,0:T(2,128)}, f32[513,513]{1,0:T(8,128)}) custom-call(f32[32,40,128]{2,1,0:T(8,128)S(1)} %get-tuple-element.9.g_ref, f32[8,128]{1,0:T(8,128)S(1)} %get-tuple-element.10.col_ref, f32[6,128]{1,0:T(8,128)S(1)} %get-tuple-element.11.f_ref, bf16[768,512]{1,0:T(8,128)(2,1)S(1)} %bitcast.9), custom_call_target="tpu_custom_call" | custom-call | tf_op jit(solution)/shard_map/factor/pallas_call | solution.py:217
Async XLA Ops:
  0.6 45.9 %copy-start = (bf16[3,1,2,128,512]{4,3,2,1,0:T(8,128)(2,1)S(1)}, bf16[3,1,2,128,512]{4,3,2,1,0:T(8,128)(2,1)}, u32[]{:S(2)}) copy-start(bf16[3,1,2,128,512]{4,3,2,1,0:T(8,128)(2,1)} %param.4) | copy-start | bytes 2359300

commit v4 on v3

--- a/solution.py
+++ b/solution.py
@@ -102,25 +102,44 @@
     return r, w
 
 
+OFF = [(b, c) for b in range(4) for c in range(b + 1, 4)]
 PAIRS = [(b, c) for b in range(4) for c in range(b, 4)]
 INDEX = {pair: i for i, pair in enumerate(PAIRS)}
 
 
-def k2_kernel(total, g_ref, col_ref, f_ref, basis_hbm, modes_hbm, mode_ref, factor_hbm, s_ref, zw_ref, zh_ref, zl_ref, basis_ref, modes_ref, factor_ref, load_s, out_s, fac_s):
+def k2_kernel(total, g_ref, col_ref, f_ref, basis_hbm, modes_hbm, mode_ref, factor_hbm, s_ref, zw_ref, zh_ref, zl_ref, basis_ref, modes_ref, factor_ref, v_ref, load_s, out_s, fac_s):
     load = pltpu.make_async_copy(basis_hbm, basis_ref, load_s)
     load.start()
     scale = 1.0 / total
-    for i in range(160):
-        s_ref[i // 16, 8 * (i % 16):8 * (i % 16) + 8, :] = g_ref[i // 5, 8 * (i % 5):8 * (i % 5) + 8, :] * scale
+    brow = lax.broadcasted_iota(jnp.int32, (B, B), 0)
+    bcol = lax.broadcasted_iota(jnp.int32, (B, B), 1)
     col = col_ref[...] * scale
     g8 = jnp.broadcast_to(jnp.concatenate([col[i:i + 1, :] for i in range(4)], axis=1), (8, 512))
-    factor_ref[...] = jnp.zeros_like(factor_ref)
-    zw_ref[...] = jnp.zeros_like(zw_ref)
-    zh_ref[...] = jnp.zeros_like(zh_ref)
-    zl_ref[...] = jnp.zeros_like(zl_ref)
+
+    def stored(i):
+        return jnp.concatenate([g_ref[4 * i + j] for j in range(4)], axis=0) * scale
+
+    def unpack(i):
+        both = stored(6 + i)
+        flip = jnp.transpose(both)
+        diag = jnp.broadcast_to(col[5 + i:6 + i, :], (B, B))
+        s_ref[INDEX[2 * i + 1, 2 * i + 1]] = jnp.where(brow == bcol, diag, jnp.where(brow > bcol, both, flip))
+        return jnp.where(brow <= bcol, both, flip)
+
+    def unpack_last():
+        s_ref[INDEX[2, 2]] = unpack(1)
+
+    def keep(i):
+        s_ref[INDEX[OFF[i]]] = stored(i)
+
+    def clear(b):
+        factor_ref[b * B:(b + 1) * B, 0:b * B] = jnp.zeros((B, b * B), F32)
+
+    factor_ref[512:513, :] = jnp.zeros((1, 513), F32)
+    v_ref[...] = jnp.zeros_like(v_ref)
     outs = []
-    later = []
-    state = [jnp.zeros((8, 512), F32), jnp.zeros((8, 1), F32)]
+    later = [functools.partial(keep, i) for i in range(6)] + [unpack_last] + [functools.partial(clear, b) for b in range(1, 4)]
+    state = [jnp.zeros((8, 1), F32)]
 
     def tick():
         if later:
@@ -147,17 +166,20 @@
         s_ref[INDEX[i, c]] = s_ref[INDEX[i, c]] - tn(panel(b, i), panel(b, c))
 
     def inverse_trail(b, i):
-        hi = (b + 1) * B
-        zw_ref[i * B:(i + 1) * B, 0:hi] = zw_ref[i * B:(i + 1) * B, 0:hi] - tn(panel(b, i), zw_ref[b * B:hi, 0:hi])
+        lo, hi = b * B, (b + 1) * B
+        part = tn(panel(b, i), zw_ref[lo:hi, 0:hi])
+        if b:
+            zw_ref[i * B:(i + 1) * B, 0:lo] = zw_ref[i * B:(i + 1) * B, 0:lo] - part[:, 0:lo]
+        zw_ref[i * B:(i + 1) * B, lo:hi] = -part[:, lo:hi]
 
     def column(b):
         lo, hi = b * B, (b + 1) * B
-        zrow = zw_ref[lo:hi, :]
-        factor_ref[lo:hi, 512:513] = nt(zrow, g8)[:, 0:1]
+        zrow = zw_ref[lo:hi, 0:hi]
+        factor_ref[lo:hi, 512:513] = nt(zrow, g8[:, 0:hi])[:, 0:1]
         start(factor_ref.at[pl.ds(lo, B)], factor_hbm.at[pl.ds(lo, B)], fac_s.at[b])
-        rrow = nt(g8, zrow)
-        state[1] = state[1] + jnp.sum(rrow * rrow, axis=1, keepdims=True)
-        state[0] = state[0] + nn(rrow, zrow)
+        rrow = nt(g8[:, 0:hi], zrow)
+        state[0] = state[0] + jnp.sum(rrow * rrow, axis=1, keepdims=True)
+        v_ref[:, 0:hi] = v_ref[:, 0:hi] + nn(rrow, zrow)
 
     def apply(b, part):
         lo, hi = b * B, (b + 1) * B
@@ -173,7 +195,7 @@
     rows = basis_ref.shape[0]
     for b in range(4):
         lo, hi = b * B, (b + 1) * B
-        r_own, w = factor_block(s_ref[INDEX[b, b]], tick)
+        r_own, w = factor_block(s_ref[INDEX[b, b]] if b else unpack(0), tick)
         while later:
             tick()
         if b < 3:
@@ -196,7 +218,7 @@
             later.append(functools.partial(column, b))
     while later:
         tick()
-    v, norm = state
+    v, norm = v_ref[...], state[0]
     d2 = col[4:5, 0:1] - norm[0:1]
     inv_d = lax.rsqrt(d2)
     factor_ref[512:513, 512:513] = d2 * inv_d
@@ -221,14 +243,14 @@
         out_specs=[pl.BlockSpec(memory_space=hbm), pl.BlockSpec(memory_space=vmem), pl.BlockSpec(memory_space=hbm)],
         scratch_shapes=[
             vmem((10, B, B), F32), vmem((512, 512), F32), vmem((512, 512), BF16), vmem((512, 512), BF16),
-            vmem((rows, 512), BF16), vmem((rows, 512), BF16), vmem((513, 513), F32), dma, dma((8,)), dma((5,)),
+            vmem((rows, 512), BF16), vmem((rows, 512), BF16), vmem((513, 513), F32), vmem((8, 512), F32), dma, dma((8,)), dma((5,)),
         ],
         compiler_params=pltpu.CompilerParams(vmem_limit_bytes=40 << 20),
         name="factor",
     )(g, col, f, basis)
 
 MESH = pl.DeviceIdType.MESH
-NPLANE, NZR, CH, CG = 16, 16, 48, 40
+NPLANE, NZR, CH = 16, 16, 32
 PIECE = CH // NZR
 NEAR = [(dx, dy) for dx in (0, 1, -1) for dy in (0, 1, -1) if (dx, dy) != (0, 0)]
 AROUND = sorted(((dx, dy) for dx in range(4) for dy in range(4) if dx or dy), key=lambda o: -(min(o[0], 4 - o[0]) + min(o[1], 4 - o[1])))
@@ -245,7 +267,7 @@
     return ahead, behind, jnp.where(sub == 0, at(16), 0.0)
 
 
-def reduce_kernel(taps_hbm, snap_hbm, basis_hbm, full_ref, col_ref, filt_ref, taps_ref, snap_ref, basis_ref, band_ref, near_out, near_in, acc, recv_a, recv_b, chunk_ref, recv_c, piece_ref, ring_ref, whole_ref, gsend, grecv, gsib, gin, gout, gz, load_s, near_s, near_r, sa, ra, sb, rb, sc, rc, sd, rd, se, re, sf, rf, sga, rga, sgb, rgb, sgc, rgc, far):
+def reduce_kernel(taps_hbm, snap_hbm, basis_hbm, full_ref, col_ref, filt_ref, taps_ref, snap_ref, basis_ref, band_ref, near_out, near_in, acc, recv_a, recv_b, chunk_ref, recv_c, piece_ref, ring_ref, whole_ref, gsend, grecv, gsib, gin, gout, gz, load_s, near_s, near_r, sa, ra, sb, rb, sc, rc, sd, rd, se, re, sf, rf, sga, rga, sgb, rgb, sgc, rgc, second, third):
     gx, gy = lax.axis_index("gx"), lax.axis_index("gy")
     x, z = gx // NZR, gx % NZR
     y, core = gy // 2, gy % 2
@@ -265,7 +287,7 @@
 
     sibling = (gx, y * 2 + (1 - core))
     barrier = pltpu.get_barrier_semaphore()
-    partners = [near_id(dx, dy) for dx, dy in NEAR] + [plane_id(o) for o in AROUND] + [z_id(k) for k in ALONG if min(k, NZR - k) <= 4] + [sibling]
+    partners = [sibling] + [plane_id(o) for o in AROUND if 0 in o] + [z_id(k) for k in (1, 2, NZR - 2, NZR - 1)]
     for partner in partners:
         pl.semaphore_signal(barrier, inc=1, device_id=partner, device_id_type=MESH)
     loads = []
@@ -281,22 +303,30 @@
     lane = lax.broadcasted_iota(jnp.int32, (8, B), 1)
     for c in loads[:3]:
         c.wait()
-    at = 0
+    own = {}
     for b in range(4):
         part = lax.dot_general(basis_ref[:, b * B:(b + 1) * B], basis_ref[:, b * B:512], (((0,), (0,)), ((), ())), preferred_element_type=F32)
-        for c in range(4 - b):
-            acc[at:at + B, :] = part[:, c * B:(c + 1) * B]
-            at += B
+        for c in range(b, 4):
+            if c == b:
+                own[b] = part[:, 0:B]
+            else:
+                at = OFF.index((b, c)) * B
+                acc[at:at + B, :] = part[:, (c - b) * B:(c - b + 1) * B]
+    brow = lax.broadcasted_iota(jnp.int32, (B, B), 0)
+    bcol = lax.broadcasted_iota(jnp.int32, (B, B), 1)
+    for i in range(2):
+        acc[768 + i * B:896 + i * B, :] = jnp.where(brow <= bcol, own[2 * i], own[2 * i + 1])
+    diag = [jnp.sum(jnp.where(brow == bcol, own[i], 0.0), axis=0, keepdims=True) for i in (1, 3)]
     pl.semaphore_wait(barrier, len(partners))
-    for k in (4, NZR - 4):
-        pl.semaphore_signal(far, inc=1, device_id=z_id(k), device_id_type=MESH)
+    for partner in partners:
+        pl.semaphore_signal(second, inc=1, device_id=partner, device_id_type=MESH)
 
     def copy(src, dst, ssem, rsem, device):
         c = pltpu.make_async_remote_copy(src_ref=src, dst_ref=dst, send_sem=ssem, recv_sem=rsem, device_id=device, device_id_type=MESH)
         c.start()
         return c
 
-    half = NPLANE * CG
+    half = NPLANE * CH
     ca = copy(acc.at[pl.ds((1 - core) * half, half)], recv_a, sa, ra, sibling)
     loads[3].wait()
     taps = taps_ref[...].astype(F32)
@@ -347,23 +377,26 @@
         if dy == -1:
             tile = jnp.where(gy == 0, 0.0, tile)
         near_out[e] = tile
-    near = [copy(near_out.at[e], near_in.at[e], near_s.at[e], near_r.at[e], near_id(dx, dy)) for e, (dx, dy) in enumerate(NEAR)]
+    pl.semaphore_wait(second, len(partners))
+    third_id = [z_id(4), z_id(NZR - 4), near_id(1, 0), near_id(-1, 0)]
+    for partner in third_id:
+        pl.semaphore_signal(third, inc=1, device_id=partner, device_id_type=MESH)
     ca.wait_recv()
     def halved(p):
-        rows = pl.ds(p * CG, CG)
-        recv_a[rows, :] = recv_a[rows, :] + acc[pl.ds(core * half + p * CG, CG), :]
+        rows = pl.ds(p * CH, CH)
+        recv_a[rows, :] = recv_a[rows, :] + acc[pl.ds(core * half + p * CH, CH), :]
     cb = []
     for e, o in enumerate(AROUND):
         p = plane_at(o)
         halved(p)
-        cb.append(copy(recv_a.at[pl.ds(p * CG, CG)], recv_b.at[e], sb.at[e], rb.at[e], plane_id(o)))
+        cb.append(copy(recv_a.at[pl.ds(p * CH, CH)], recv_b.at[e], sb.at[e], rb.at[e], plane_id(o)))
     halved(plane)
-    total = recv_a[pl.ds(plane * CG, CG), :]
+    pl.semaphore_wait(third, len(third_id))
+    near = [copy(near_out.at[e], near_in.at[e], near_s.at[e], near_r.at[e], near_id(dx, dy)) for e, (dx, dy) in enumerate(NEAR)]
+    total = recv_a[pl.ds(plane * CH, CH), :]
     for e in reversed(range(NPLANE - 1)):
         cb[e].wait_recv()
         total = total + recv_b[e]
-    pl.semaphore_wait(far, 2)
-    total = jnp.concatenate([total, jnp.zeros((CH - CG, B), F32)], axis=0)
     for i in range(NZR):
         chunk_ref[i] = total[i * PIECE:(i + 1) * PIECE, :]
     cc = []
@@ -382,6 +415,8 @@
     sq = jnp.where(sub < 6, f * f, 0.0)
     ff = jnp.sum(jnp.sum(sq, axis=1, keepdims=True), axis=0, keepdims=True)
     tail = jnp.where(sub == 4, jnp.broadcast_to(ff, (8, B)), 0.0)
+    for i in range(2):
+        tail = jnp.where(sub == 5 + i, jnp.broadcast_to(diag[i], (8, B)), tail)
     for i in range(4):
         tail = jnp.where(sub == i, g[:, i * B:(i + 1) * B], tail)
     gsend[...] = tail
@@ -410,14 +445,14 @@
         c.wait_recv()
     for i in range(NZR):
         whole_ref[i * PIECE:(i + 1) * PIECE, :] = ring_ref[i]
-    rows = pl.ds(0, CG)
+    rows = pl.ds(0, CH)
     def slot(c, p):
         return full_ref.at[c * NPLANE + p, rows]
     ce = []
     for e, o in enumerate(AROUND):
         ce.append(copy(whole_ref.at[rows], slot(core, plane), se.at[e], re.at[e], plane_id(o)))
     cf = [copy(whole_ref.at[rows], slot(core, plane), sf.at[NPLANE - 1], rf.at[NPLANE - 1], sibling)]
-    full_ref[core * NPLANE + plane] = whole_ref[0:CG, :]
+    full_ref[core * NPLANE + plane] = whole_ref[...]
     for e in reversed(range(NPLANE - 1)):
         ce[e].wait_recv()
         p = plane_at((4 - AROUND[e][0], 4 - AROUND[e][1]))
@@ -440,7 +475,7 @@
     n = NPLANE - 1
     return pl.pallas_call(
         reduce_kernel,
-        out_shape=(jax.ShapeDtypeStruct((2 * NPLANE, CG, B), F32), jax.ShapeDtypeStruct((8, B), F32), jax.ShapeDtypeStruct((6, B), F32)),
+        out_shape=(jax.ShapeDtypeStruct((2 * NPLANE, CH, B), F32), jax.ShapeDtypeStruct((8, B), F32), jax.ShapeDtypeStruct((6, B), F32)),
         in_specs=[pl.BlockSpec(memory_space=pltpu.HBM)] * 3,
         out_specs=[pl.BlockSpec(memory_space=vmem)] * 3,
         scratch_shapes=[
@@ -450,9 +485,9 @@
             vmem((1024, B), BF16),
             vmem((8, 8, B), F32),
             vmem((8, 8, B), F32),
-            vmem((2 * NPLANE * CG, B), F32),
-            vmem((NPLANE * CG, B), F32),
-            vmem((n, CG, B), F32),
+            vmem((2 * NPLANE * CH, B), F32),
+            vmem((NPLANE * CH, B), F32),
+            vmem((n, CH, B), F32),
             vmem((NZR, PIECE, B), F32),
             vmem((n, PIECE, B), F32),
             vmem((PIECE, B), F32),
@@ -466,7 +501,7 @@
             vmem((NZR, 8, B), F32),
             dma((7,)), dma((8,)), dma((8,)), dma, dma,
             dma((n,)), dma((n,)), dma((n,)), dma((n,)), dma((n,)), dma((n,)), dma((n,)), dma((n,)), dma((n + 1,)), dma((n + 1,)),
-            dma, dma, dma((n,)), dma((n,)), dma((n,)), dma((n,)), pltpu.SemaphoreType.REGULAR,
+            dma, dma, dma((n,)), dma((n,)), dma((n,)), dma((n,)), pltpu.SemaphoreType.REGULAR, pltpu.SemaphoreType.REGULAR,
         ],
         compiler_params=pltpu.CompilerParams(vmem_limit_bytes=40<<20, collective_id=0, has_side_effects=True),
         name="reduce",

time: 62.2 us -> 60.3 us (0.969)
  Pallas kernels: 61.3 us -> 59.4 us
    pallas_call x1, Pallas kernels: 45.9 us -> 44 us  [reduced(): pl.pallas_call(reduce_kernel, out_shape=(jax.ShapeDtypeStruct((2 * NPLANE...]
where the time goes in v4:
time: 60.3 us; the launch traced here: 60.2 us
  Pallas kernels  59.4 us (99%)
  between operations  0.81 us (1%)
    pallas_call x1, Pallas kernels, reduced(): pl.pallas_call(reduce_kernel, out_shape=(jax.ShapeDtypeStruct((2 * NPLANE...  44 us
    pallas_call x1, Pallas kernels, k2(): pl.pallas_call(functools.partial(k2_kernel, total), out_shape=(jax.ShapeD...  15.4 us

profile of v4, /device:TPU:1, one launch (start us, length us, event | category | flops | bytes accessed | tf_op | source)
XLA Modules:
  0.0 60.2 jit_solution(15663534088731424454)
XLA Ops:
  0.6 0.0 copy-start
  0.6 44.0 %reduce.1 = (f32[32,32,128]{2,1,0:T(8,128)S(1)}, f32[8,128]{1,0:T(8,128)S(1)}, f32[6,128]{1,0:T(8,128)S(1)}) custom-call(bf16[3,17]{1,0:T(4,128)(2,1)} %taps_hbm.1, bf16[384,1024]{1,0:T(8,128)(2,1)} %bitcast.10, bf16[768,512]{1,0:T(8,128)(2,1)} %bitcast.8), custom_call_target="tpu_custom_call" | custom-call | tf_op jit(solution)/shard_map/reduce/pallas_call | solution.py:476
  44.6 0.0 copy-done
  44.6 15.4 %factor.1 = (bf16[768,512]{1,0:T(8,128)(2,1)}, f32[3,2,128]{2,1,0:T(2,128)}, f32[513,513]{1,0:T(8,128)}) custom-call(f32[32,32,128]{2,1,0:T(8,128)S(1)} %get-tuple-element.9.g_ref, f32[8,128]{1,0:T(8,128)S(1)} %get-tuple-element.10.col_ref, f32[6,128]{1,0:T(8,128)S(1)} %get-tuple-element.11.f_ref, bf16[768,512]{1,0:T(8,128)(2,1)S(1)} %bitcast.9), custom_call_target="tpu_custom_call" | custom-call | tf_op jit(solution)/shard_map/factor/pallas_call | solution.py:239
Async XLA Ops:
  0.6 44.0 %copy-start = (bf16[3,1,2,128,512]{4,3,2,1,0:T(8,128)(2,1)S(1)}, bf16[3,1,2,128,512]{4,3,2,1,0:T(8,128)(2,1)}, u32[]{:S(2)}) copy-start(bf16[3,1,2,128,512]{4,3,2,1,0:T(8,128)(2,1)} %param.4) | copy-start | bytes 2359300

commit v5 on v4

--- a/solution.py
+++ b/solution.py
@@ -107,7 +107,7 @@
 INDEX = {pair: i for i, pair in enumerate(PAIRS)}
 
 
-def k2_kernel(total, g_ref, col_ref, f_ref, basis_hbm, modes_hbm, mode_ref, factor_hbm, s_ref, zw_ref, zh_ref, zl_ref, basis_ref, modes_ref, factor_ref, v_ref, load_s, out_s, fac_s):
+def k2_kernel(total, g_ref, col_ref, f_ref, basis_hbm, modes_hbm, mode_hbm, factor_hbm, s_ref, zw_ref, zh_ref, zl_ref, basis_ref, modes_ref, factor_ref, v_ref, c_ref, mode_ref, load_s, out_s, fac_s):
     load = pltpu.make_async_copy(basis_hbm, basis_ref, load_s)
     load.start()
     scale = 1.0 / total
@@ -137,9 +137,10 @@
 
     factor_ref[512:513, :] = jnp.zeros((1, 513), F32)
     v_ref[...] = jnp.zeros_like(v_ref)
+    c_ref[...] = g8
     outs = []
     later = [functools.partial(keep, i) for i in range(6)] + [unpack_last] + [functools.partial(clear, b) for b in range(1, 4)]
-    state = [jnp.zeros((8, 1), F32)]
+    state = [jnp.zeros((8, 1), F32), None]
 
     def tick():
         if later:
@@ -172,14 +173,20 @@
             zw_ref[i * B:(i + 1) * B, 0:lo] = zw_ref[i * B:(i + 1) * B, 0:lo] - part[:, 0:lo]
         zw_ref[i * B:(i + 1) * B, lo:hi] = -part[:, lo:hi]
 
-    def column(b):
+    def column(b, w):
         lo, hi = b * B, (b + 1) * B
-        zrow = zw_ref[lo:hi, 0:hi]
-        factor_ref[lo:hi, 512:513] = nt(zrow, g8[:, 0:hi])[:, 0:1]
+        c = c_ref[:, lo:hi]
+        factor_ref[lo:hi, 512:513] = nt(w, c)[:, 0:1]
         start(factor_ref.at[pl.ds(lo, B)], factor_hbm.at[pl.ds(lo, B)], fac_s.at[b])
-        rrow = nt(g8[:, 0:hi], zrow)
-        state[0] = state[0] + jnp.sum(rrow * rrow, axis=1, keepdims=True)
-        v_ref[:, 0:hi] = v_ref[:, 0:hi] + nn(rrow, zrow)
+        r = nt(c, w)
+        for i in range(b + 1, 4):
+            c_ref[:, i * B:(i + 1) * B] = c_ref[:, i * B:(i + 1) * B] - nn(r, panel(b, i))
+        state[0] = state[0] + jnp.sum(r * r, axis=1, keepdims=True)
+        state[1] = r
+
+    def back(b):
+        hi = (b + 1) * B
+        v_ref[:, 0:hi] = v_ref[:, 0:hi] + nn(state[1], zw_ref[b * B:hi, 0:hi])
 
     def apply(b, part):
         lo, hi = b * B, (b + 1) * B
@@ -204,18 +211,16 @@
         factor_ref[lo:hi, lo:hi] = r_own
         for c in range(b + 2, 4):
             later.append(functools.partial(factor_off, b, c, w))
+        later.append(functools.partial(column, b, w))
         later.append(functools.partial(inverse_row, b, w))
+        later.append(functools.partial(back, b))
         for i in range(b + 1, 4):
             for c in range(i, 4):
                 if (i, c) != (b + 1, b + 1):
                     later.append(functools.partial(trail, b, i, c))
             later.append(functools.partial(inverse_trail, b, i))
-        if b < 3:
-            later.append(functools.partial(column, b))
         later.append(functools.partial(apply, b, 0))
         later.append(functools.partial(apply, b, 1))
-        if b == 3:
-            later.append(functools.partial(column, b))
     while later:
         tick()
     v, norm = v_ref[...], state[0]
@@ -229,6 +234,7 @@
     f = f_ref[...]
     for i in range(6):
         mode_ref[i // 2, i % 2:i % 2 + 1, :] = (f[i:i + 1, :] - y[0:1, i * B:(i + 1) * B]) * inv_d
+    start(mode_ref, mode_hbm, fac_s.at[5])
     for c in outs:
         c.wait()
 
@@ -240,10 +246,10 @@
         functools.partial(k2_kernel, total),
         out_shape=(jax.ShapeDtypeStruct((rows, 512), BF16), jax.ShapeDtypeStruct((3, 2, B), F32), jax.ShapeDtypeStruct((513, 513), F32)),
         in_specs=[pl.BlockSpec(memory_space=vmem)] * 3 + [pl.BlockSpec(memory_space=hbm)],
-        out_specs=[pl.BlockSpec(memory_space=hbm), pl.BlockSpec(memory_space=vmem), pl.BlockSpec(memory_space=hbm)],
+        out_specs=[pl.BlockSpec(memory_space=hbm)] * 3,
         scratch_shapes=[
             vmem((10, B, B), F32), vmem((512, 512), F32), vmem((512, 512), BF16), vmem((512, 512), BF16),
-            vmem((rows, 512), BF16), vmem((rows, 512), BF16), vmem((513, 513), F32), vmem((8, 512), F32), dma, dma((8,)), dma((5,)),
+            vmem((rows, 512), BF16), vmem((rows, 512), BF16), vmem((513, 513), F32), vmem((8, 512), F32), vmem((8, 512), F32), vmem((3, 2, B), F32), dma, dma((8,)), dma((6,)),
         ],
         compiler_params=pltpu.CompilerParams(vmem_limit_bytes=40 << 20),
         name="factor",
@@ -505,11 +511,11 @@
         ],
         compiler_params=pltpu.CompilerParams(vmem_limit_bytes=40<<20, collective_id=0, has_side_effects=True),
         name="reduce",
-    )(*(pltpu.with_memory_space_constraint(v, pltpu.HBM) for v in (taps, snap, basis)))
+    )(pltpu.with_memory_space_constraint(taps, pltpu.HBM), pltpu.with_memory_space_constraint(snap, pltpu.HBM), basis)
 
 
 def local(snapshot, basis, taps):
-    flat = basis.reshape(-1, basis.shape[-1])
+    flat = pltpu.with_memory_space_constraint(basis.reshape(-1, basis.shape[-1]), pltpu.HBM)
     g, col, f = reduced(taps, snapshot.reshape(-1, snapshot.shape[-1]), flat)
     total = flat.shape[0] * lax.axis_size("gx") * lax.axis_size("gy")
     modes, mode, fac = k2(g, col, f, flat, float(total))

time: 60.3 us -> 60.2 us (level)
  no operation moved by 1% of the time
where the time goes in v5:
time: 60.2 us; the launch traced here: 60 us
  Pallas kernels  59.2 us (98%)
  between operations  0.8 us (1%)
    pallas_call x1, Pallas kernels, reduced(): pl.pallas_call(reduce_kernel, out_shape=(jax.ShapeDtypeStruct((2 * NPLANE...  43.8 us
    pallas_call x1, Pallas kernels, k2(): pl.pallas_call(functools.partial(k2_kernel, total), out_shape=(jax.ShapeD...  15.4 us

profile of v5, /device:TPU:1, one launch (start us, length us, event | category | flops | bytes accessed | tf_op | source)
XLA Modules:
  0.0 60.0 jit_solution(10209177485077049934)
XLA Ops:
  0.6 43.8 %reduce.1 = (f32[32,32,128]{2,1,0:T(8,128)S(1)}, f32[8,128]{1,0:T(8,128)S(1)}, f32[6,128]{1,0:T(8,128)S(1)}) custom-call(bf16[3,17]{1,0:T(4,128)(2,1)} %taps_hbm.1, bf16[384,1024]{1,0:T(8,128)(2,1)} %bitcast.10, bf16[768,512]{1,0:T(8,128)(2,1)} %bitcast.8), custom_call_target="tpu_custom_call" | custom-call | tf_op jit(solution)/shard_map/reduce/pallas_call | solution.py:482
  44.5 15.4 %factor.1 = (bf16[768,512]{1,0:T(8,128)(2,1)}, f32[3,2,128]{2,1,0:T(2,128)}, f32[513,513]{1,0:T(8,128)}) custom-call(f32[32,32,128]{2,1,0:T(8,128)S(1)} %get-tuple-element.9.g_ref, f32[8,128]{1,0:T(8,128)S(1)} %get-tuple-element.10.col_ref, f32[6,128]{1,0:T(8,128)S(1)} %get-tuple-element.11.f_ref, bf16[768,512]{1,0:T(8,128)(2,1)} %bitcast.9), custom_call_target="tpu_custom_call" | custom-call | tf_op jit(solution)/shard_map/factor/pallas_call | solution.py:245
